TPU v7x, 128 devices: a whole 4x4x4 slice. The times are simulated.
128 devices in a mesh: user: 16 (over y, z), item: 8 (over x, core).
Axes of the slice: x: 4, y: 4, z: 4, core: 2. Of those that a mesh axis runs over, the one named last changes fastest.
Arguments:
- theta_shape: float32 [32768, 1024], P('user', 'item'), may hold values from 0.3 to 3
- theta_rate: float32 [32768, 1024], P('user', 'item'), may hold values from 100 to 1000
- xi_rate: float32 [32768], P('user'), may hold values from 1 to 10
- beta_shape: float32 [8192, 1024], P('item', 'user'), may hold values from 0.3 to 3
- beta_rate: float32 [8192, 1024], P('item', 'user'), may hold values from 50 to 500
- eta_rate: float32 [8192], P('item'), may hold values from 1 to 10
- tile_slots: int32 [16, 8, 32], P('user', 'item'), may hold values from 0 to 31, as said below
- tile_counts: bfloat16 [16, 8, 32, 256, 256], P('user', 'item'), may hold values from 0 to 5, as said below
- live_tiles: int32 [16, 8], P('user', 'item'), may hold values from 1 to 32, as said below
Outputs:
- theta_shape_new: float32 [32768, 1024], P('user', 'item')
- theta_log_rate: float32 [32768, 1024], P('user', 'item')
- xi_rate_new: float32 [32768], P('user')
- beta_shape_new: float32 [8192, 1024], P('item', 'user')
- beta_log_rate: float32 [8192, 1024], P('item', 'user')
- eta_rate_new: float32 [8192], P('item')
Inputs may be any that keep to these rules, and one draw needn't show every extreme that they name: `tile_slots`: within one device's 32 slots the positions are distinct. `tile_counts`: whole numbers. `live_tiles`: some device uses all 32 slots.
All inputs are finite; a program needn't handle non-finite values.
Results may differ from a plain program's by a relative error of at most 0.0029.
Values may be sent and summed in bfloat16 or wider, within the bound.
A program may use at most 128 MiB of HBM per device.

v0:
```python
import math

import jax
import jax.numpy as jnp
from jax import lax
from jax.sharding import PartitionSpec as P

BLK = 256
UB = 8
IB = 4
TMAX = 32


prior_a = 0.3
prior_a2 = 0.3
prior_b2 = 1.0
prior_c = 0.3
prior_c2 = 0.3
prior_d2 = 1.0


def exp_mean_log(shape_param, rate_param):
    return jnp.exp(lax.digamma(shape_param) - jnp.log(rate_param)).astype(jnp.bfloat16)


def on_device(
    theta_shape,
    theta_rate,
    xi_rate,
    beta_shape,
    beta_rate,
    eta_rate,
    tile_slots,
    tile_counts,
    live_tiles,
):
    user_width = lax.axis_size("user")
    item_width = lax.axis_size("item")
    user_index = lax.axis_index("user")
    item_index = lax.axis_index("item")
    theta_part = exp_mean_log(theta_shape, theta_rate)
    beta_part = exp_mean_log(beta_shape, beta_rate)
    theta_full = lax.all_gather(theta_part, "item", axis=1, tiled=True)
    beta_full = lax.all_gather(beta_part, "user", axis=1, tiled=True)
    factors = theta_full.shape[1]
    user_rows = theta_full.shape[0]
    item_rows = beta_full.shape[0]
    theta_blocks = theta_full.reshape(UB, BLK, factors)
    beta_blocks = beta_full.reshape(IB, BLK, factors)
    slot_list = tile_slots.reshape(TMAX)
    count_tiles = tile_counts.reshape(TMAX, BLK, BLK)
    used_slots = live_tiles.reshape(())
    user_blocks = slot_list // IB
    item_blocks = slot_list % IB
    group_size = math.gcd(TMAX, 8)

    def group_step(group_index, carried):
        user_acc, item_acc = carried
        first_slot = group_index * group_size
        rows_user = lax.dynamic_slice_in_dim(user_blocks, first_slot, group_size, 0)
        rows_item = lax.dynamic_slice_in_dim(item_blocks, first_slot, group_size, 0)
        counts = lax.dynamic_slice_in_dim(count_tiles, first_slot, group_size, 0).astype(
            jnp.float32
        )
        slot_mask = (first_slot + jnp.arange(group_size) < used_slots).astype(jnp.float32)
        counts = counts * slot_mask[:, None, None]
        users = jnp.take(theta_blocks, rows_user, axis=0)
        items = jnp.take(beta_blocks, rows_item, axis=0)
        denominator = jnp.einsum("tuk,tik->tui", users, items, preferred_element_type=jnp.float32)
        ratio_tile = (counts / denominator).astype(jnp.bfloat16)
        user_terms = jnp.einsum(
            "tui,tik->tuk", ratio_tile, items, preferred_element_type=jnp.float32
        )
        item_terms = jnp.einsum(
            "tui,tuk->tik", ratio_tile, users, preferred_element_type=jnp.float32
        )
        user_acc = user_acc.at[rows_user].add(user_terms)
        item_acc = item_acc.at[rows_item].add(item_terms)
        return (user_acc, item_acc)

    start_acc = (
        jnp.zeros((UB, BLK, factors), jnp.float32),
        jnp.zeros((IB, BLK, factors), jnp.float32),
    )
    group_count = TMAX // group_size
    user_acc, item_acc = lax.fori_loop(0, group_count, group_step, start_acc)
    user_acc = user_acc.reshape(user_rows, factors)
    item_acc = item_acc.reshape(item_rows, factors)
    beta_columns = factors // user_width
    theta_columns = factors // item_width
    beta_local = jnp.sum(beta_shape / beta_rate, axis=0)
    theta_local = jnp.sum(theta_shape / theta_rate, axis=0)
    beta_placed = lax.dynamic_update_slice_in_dim(
        jnp.zeros((factors,), jnp.float32), beta_local, user_index * beta_columns, 0
    )
    theta_placed = lax.dynamic_update_slice_in_dim(
        jnp.zeros((factors,), jnp.float32), theta_local, item_index * theta_columns, 0
    )
    beta_total, theta_total = lax.psum((beta_placed, theta_placed), ("user", "item"))
    xi_mean = (prior_a2 + factors * prior_a) / xi_rate
    user_summed = lax.psum(user_acc, "item")
    shape_whole = prior_a + theta_full.astype(jnp.float32) * user_summed
    rate_whole = xi_mean[:, None] + beta_total[None, :]
    xi_rate_new = prior_a2 / prior_b2 + jnp.sum(shape_whole / rate_whole, axis=1)
    theta_shape_new = lax.dynamic_slice_in_dim(
        shape_whole, item_index * theta_columns, theta_columns, 1
    )
    theta_rate_new = lax.dynamic_slice_in_dim(
        rate_whole, item_index * theta_columns, theta_columns, 1
    )
    item_share = lax.psum_scatter(item_acc, "user", scatter_dimension=1, tiled=True)
    beta_shape_new = prior_c + beta_part.astype(jnp.float32) * item_share
    eta_mean = (prior_c2 + factors * prior_c) / eta_rate
    theta_slice = lax.dynamic_slice_in_dim(theta_total, user_index * beta_columns, beta_columns, 0)
    beta_rate_new = eta_mean[:, None] + theta_slice[None, :]
    item_part = jnp.sum(beta_shape_new / beta_rate_new, axis=1)
    eta_rate_new = prior_c2 / prior_d2 + lax.psum(item_part, "user")
    return (
        theta_shape_new,
        jnp.log(theta_rate_new),
        xi_rate_new,
        beta_shape_new,
        jnp.log(beta_rate_new),
        eta_rate_new,
    )


def solution(mesh):
    in_specs = (
        P("user", "item"),
        P("user", "item"),
        P("user"),
        P("item", "user"),
        P("item", "user"),
        P("item"),
        P("user", "item", None),
        P("user", "item", None, None, None),
        P("user", "item"),
    )
    out_specs = (
        P("user", "item"),
        P("user", "item"),
        P("user"),
        P("item", "user"),
        P("item", "user"),
        P("item"),
    )
    return jax.shard_map(
        on_device, mesh=mesh, in_specs=in_specs, out_specs=out_specs, check_vma=False
    )
```

profile of v0, /device:TPU:0, one launch (start us, length us, event | category | flops | bytes accessed | tf_op | source)
XLA Modules:
  0.0 585.9 jit_solution(17725922907850720413)
XLA Ops:
  7.2 4.1 fusion.22
  11.4 9.8 %fusion.16 = (bf16[2048,128]{1,0:T(8,128)(2,1)}, f32[128]{0:T(128)}) fusion(f32[2048,128]{1,0:T(8,128)} %param.12, f32[2048,128]{1,0:T(8,128)} %param.11), kind=kLoop, calls=%fused_computation.36 | loop fusion | flops 20709248 | bytes 2621952 | tf_op jit(solution)/shard_map/convert_element_type | solution.py:23
  22.0 37.3 %all-gather.5.cloned.1.call-done = bf16[1024,1024]{0,1:T(8,128)(2,1)} async-done(((bf16[1024,64]{0,1:T(8,128)(2,1)}), bf16[1024,1024]{0,1:T(8,128)(2,1)}) %all-gather.5.cloned.1.call-update) | async-done | bytes 2097168 | tf_op jit(solution)/shard_map/all_gather | solution.py:44
  59.3 2.9 copy.19
  62.2 34.7 %all-gather.3.cloned.1.call-done = bf16[2048,1024]{1,0:T(8,128)(2,1)} async-done(((bf16[2048,128]{1,0:T(8,128)(2,1)}), bf16[2048,1024]{1,0:T(8,128)(2,1)}) %all-gather.3.cloned.1.call-update) | async-done | bytes 4194320 | tf_op jit(solution)/shard_map/all_gather | solution.py:43
  96.8 4.3 broadcast_in_dim.57
  101.1 2.5 broadcast_in_dim.58
  103.6 247.2 %while.15 = (s32[]{:T(128)}, f32[8,256,1024]{2,1,0:T(8,128)}, f32[4,256,1024]{2,1,0:T(8,128)}, s32[32]{0:T(128)S(1)}, bf16[32,256,256]{2,1,0:T(8,128)(2,1)}, /*i...) while((s32[]{:T(128)}, f32[8,256,1024]{2,1,0:T(8,128)}, ...), condition=%wide.region_3.4_spmd, body=%wide.region_0.3_spmd.sunk | while | flops 3238004736 | bytes 134226640 | solution.py:86
  103.7 4.9 gather_fusion
  108.6 2.8 gather_fusion.1
  111.4 5.0 fusion.28
  116.5 0.7 compare_convert_fusion.2
  117.2 6.0 %fusion.30 = f32[8,256,1024]{2,1,0:T(8,128)} fusion(f32[8,256,256]{2,1,0:T(8,128)S(1)} %fusion.28, bf16[8,256,1024]{2,1,0:T(8,128)(2,1)S(1)} %copy-done, pred[8]{0:T(512)(128)(4,1)S(1)} %get-tuple-element.272, f32[8]{0:T(128)S(1)} %compare_convert_fusion.2, bf16[32,256,256]{2,1,0:T(8,128)(2,1)} %get-tuple-element.305, s32[]{:T(128)S(6)} %select_n.90), kind=kOutput, calls=%fused_computation.7.clone.1 | convolution fusion | flops 1077936128 | bytes 15728684 | tf_op jit(solution)/shard_map/while/body/eval_jaxpr/tui,tuk->tik/dot_general | solution.py:74
  123.2 17.1 %scatter_fusion.1 = f32[4,256,1024]{2,1,0:T(8,128)} fusion(f32[4,256,1024]{2,1,0:T(8,128)} %get-tuple-element.290, s32[8]{0:T(128)S(1)} %get-tuple-element.273, f32[8,256,1024]{2,1,0:T(8,128)} %fusion.30), kind=kCustom, calls=%fused_computation.3.clone.1 | custom fusion | flops 2097152 | bytes 25165856 | tf_op jit(solution)/shard_map/while/body/eval_jaxpr/scatter-add | solution.py:78
  140.3 7.7 %fusion.29 = f32[8,256,1024]{2,1,0:T(8,128)} fusion(f32[8,256,256]{2,1,0:T(8,128)} %copy-done.6, bf16[8,256,1024]{2,1,0:T(8,128)(2,1)} %gather_fusion.1, pred[8]{0:T(512)(128)(4,1)S(1)} %get-tuple-element.274, f32[8]{0:T(128)S(1)} %compare_convert_fusion.2, bf16[32,256,256]{2,1,0:T(8,128)(2,1)} %get-tuple-element.305, s32[]{:T(128)S(6)} %select_n.90), kind=kOutput, calls=%fused_computation.8.clone.1 | convolution fusion | flops 1077936128 | bytes 15728684 | tf_op jit(solution)/shard_map/while/body/eval_jaxpr/tui,tik->tuk/dot_general | solution.py:71
  148.0 17.2 %scatter_fusion = f32[8,256,1024]{2,1,0:T(8,128)} fusion(f32[8,256,1024]{2,1,0:T(8,128)} %get-tuple-element.289, s32[8]{0:T(128)S(1)} %get-tuple-element.271, f32[8,256,1024]{2,1,0:T(8,128)} %fusion.29), kind=kCustom, calls=%fused_computation.2.clone.1 | custom fusion | flops 2097152 | bytes 25165856 | tf_op jit(solution)/shard_map/while/body/eval_jaxpr/scatter-add | solution.py:77
  165.2 4.9 gather_fusion
  170.2 2.8 gather_fusion.1
  173.0 5.0 fusion.28
  178.0 0.7 compare_convert_fusion.2
  178.7 6.0 %fusion.30 = f32[8,256,1024]{2,1,0:T(8,128)} fusion(f32[8,256,256]{2,1,0:T(8,128)S(1)} %fusion.28, bf16[8,256,1024]{2,1,0:T(8,128)(2,1)S(1)} %copy-done, pred[8]{0:T(512)(128)(4,1)S(1)} %get-tuple-element.272, f32[8]{0:T(128)S(1)} %compare_convert_fusion.2, bf16[32,256,256]{2,1,0:T(8,128)(2,1)} %get-tuple-element.305, s32[]{:T(128)S(6)} %select_n.90), kind=kOutput, calls=%fused_computation.7.clone.1 | convolution fusion | flops 1077936128 | bytes 15728684 | tf_op jit(solution)/shard_map/while/body/eval_jaxpr/tui,tuk->tik/dot_general | solution.py:74
  184.7 17.0 %scatter_fusion.1 = f32[4,256,1024]{2,1,0:T(8,128)} fusion(f32[4,256,1024]{2,1,0:T(8,128)} %get-tuple-element.290, s32[8]{0:T(128)S(1)} %get-tuple-element.273, f32[8,256,1024]{2,1,0:T(8,128)} %fusion.30), kind=kCustom, calls=%fused_computation.3.clone.1 | custom fusion | flops 2097152 | bytes 25165856 | tf_op jit(solution)/shard_map/while/body/eval_jaxpr/scatter-add | solution.py:78
  201.7 7.7 %fusion.29 = f32[8,256,1024]{2,1,0:T(8,128)} fusion(f32[8,256,256]{2,1,0:T(8,128)} %copy-done.6, bf16[8,256,1024]{2,1,0:T(8,128)(2,1)} %gather_fusion.1, pred[8]{0:T(512)(128)(4,1)S(1)} %get-tuple-element.274, f32[8]{0:T(128)S(1)} %compare_convert_fusion.2, bf16[32,256,256]{2,1,0:T(8,128)(2,1)} %get-tuple-element.305, s32[]{:T(128)S(6)} %select_n.90), kind=kOutput, calls=%fused_computation.8.clone.1 | convolution fusion | flops 1077936128 | bytes 15728684 | tf_op jit(solution)/shard_map/while/body/eval_jaxpr/tui,tik->tuk/dot_general | solution.py:71
  209.5 17.2 %scatter_fusion = f32[8,256,1024]{2,1,0:T(8,128)} fusion(f32[8,256,1024]{2,1,0:T(8,128)} %get-tuple-element.289, s32[8]{0:T(128)S(1)} %get-tuple-element.271, f32[8,256,1024]{2,1,0:T(8,128)} %fusion.29), kind=kCustom, calls=%fused_computation.2.clone.1 | custom fusion | flops 2097152 | bytes 25165856 | tf_op jit(solution)/shard_map/while/body/eval_jaxpr/scatter-add | solution.py:77
  226.7 4.9 gather_fusion
  231.6 2.8 gather_fusion.1
  234.4 5.0 fusion.28
  239.5 0.7 compare_convert_fusion.2
  240.2 6.0 %fusion.30 = f32[8,256,1024]{2,1,0:T(8,128)} fusion(f32[8,256,256]{2,1,0:T(8,128)S(1)} %fusion.28, bf16[8,256,1024]{2,1,0:T(8,128)(2,1)S(1)} %copy-done, pred[8]{0:T(512)(128)(4,1)S(1)} %get-tuple-element.272, f32[8]{0:T(128)S(1)} %compare_convert_fusion.2, bf16[32,256,256]{2,1,0:T(8,128)(2,1)} %get-tuple-element.305, s32[]{:T(128)S(6)} %select_n.90), kind=kOutput, calls=%fused_computation.7.clone.1 | convolution fusion | flops 1077936128 | bytes 15728684 | tf_op jit(solution)/shard_map/while/body/eval_jaxpr/tui,tuk->tik/dot_general | solution.py:74
  246.2 17.6 %scatter_fusion.1 = f32[4,256,1024]{2,1,0:T(8,128)} fusion(f32[4,256,1024]{2,1,0:T(8,128)} %get-tuple-element.290, s32[8]{0:T(128)S(1)} %get-tuple-element.273, f32[8,256,1024]{2,1,0:T(8,128)} %fusion.30), kind=kCustom, calls=%fused_computation.3.clone.1 | custom fusion | flops 2097152 | bytes 25165856 | tf_op jit(solution)/shard_map/while/body/eval_jaxpr/scatter-add | solution.py:78
  263.7 7.7 %fusion.29 = f32[8,256,1024]{2,1,0:T(8,128)} fusion(f32[8,256,256]{2,1,0:T(8,128)} %copy-done.6, bf16[8,256,1024]{2,1,0:T(8,128)(2,1)} %gather_fusion.1, pred[8]{0:T(512)(128)(4,1)S(1)} %get-tuple-element.274, f32[8]{0:T(128)S(1)} %compare_convert_fusion.2, bf16[32,256,256]{2,1,0:T(8,128)(2,1)} %get-tuple-element.305, s32[]{:T(128)S(6)} %select_n.90), kind=kOutput, calls=%fused_computation.8.clone.1 | convolution fusion | flops 1077936128 | bytes 15728684 | tf_op jit(solution)/shard_map/while/body/eval_jaxpr/tui,tik->tuk/dot_general | solution.py:71
  271.4 17.5 %scatter_fusion = f32[8,256,1024]{2,1,0:T(8,128)} fusion(f32[8,256,1024]{2,1,0:T(8,128)} %get-tuple-element.289, s32[8]{0:T(128)S(1)} %get-tuple-element.271, f32[8,256,1024]{2,1,0:T(8,128)} %fusion.29), kind=kCustom, calls=%fused_computation.2.clone.1 | custom fusion | flops 2097152 | bytes 25165856 | tf_op jit(solution)/shard_map/while/body/eval_jaxpr/scatter-add | solution.py:77
  289.0 4.9 gather_fusion
  293.9 2.8 gather_fusion.1
  296.7 5.0 fusion.28
  301.8 0.7 compare_convert_fusion.2
  302.5 6.0 %fusion.30 = f32[8,256,1024]{2,1,0:T(8,128)} fusion(f32[8,256,256]{2,1,0:T(8,128)S(1)} %fusion.28, bf16[8,256,1024]{2,1,0:T(8,128)(2,1)S(1)} %copy-done, pred[8]{0:T(512)(128)(4,1)S(1)} %get-tuple-element.272, f32[8]{0:T(128)S(1)} %compare_convert_fusion.2, bf16[32,256,256]{2,1,0:T(8,128)(2,1)} %get-tuple-element.305, s32[]{:T(128)S(6)} %select_n.90), kind=kOutput, calls=%fused_computation.7.clone.1 | convolution fusion | flops 1077936128 | bytes 15728684 | tf_op jit(solution)/shard_map/while/body/eval_jaxpr/tui,tuk->tik/dot_general | solution.py:74
  308.5 17.2 %scatter_fusion.1 = f32[4,256,1024]{2,1,0:T(8,128)} fusion(f32[4,256,1024]{2,1,0:T(8,128)} %get-tuple-element.290, s32[8]{0:T(128)S(1)} %get-tuple-element.273, f32[8,256,1024]{2,1,0:T(8,128)} %fusion.30), kind=kCustom, calls=%fused_computation.3.clone.1 | custom fusion | flops 2097152 | bytes 25165856 | tf_op jit(solution)/shard_map/while/body/eval_jaxpr/scatter-add | solution.py:78
  325.7 7.7 %fusion.29 = f32[8,256,1024]{2,1,0:T(8,128)} fusion(f32[8,256,256]{2,1,0:T(8,128)} %copy-done.6, bf16[8,256,1024]{2,1,0:T(8,128)(2,1)} %gather_fusion.1, pred[8]{0:T(512)(128)(4,1)S(1)} %get-tuple-element.274, f32[8]{0:T(128)S(1)} %compare_convert_fusion.2, bf16[32,256,256]{2,1,0:T(8,128)(2,1)} %get-tuple-element.305, s32[]{:T(128)S(6)} %select_n.90), kind=kOutput, calls=%fused_computation.8.clone.1 | convolution fusion | flops 1077936128 | bytes 15728684 | tf_op jit(solution)/shard_map/while/body/eval_jaxpr/tui,tik->tuk/dot_general | solution.py:71
  333.4 17.4 %scatter_fusion = f32[8,256,1024]{2,1,0:T(8,128)} fusion(f32[8,256,1024]{2,1,0:T(8,128)} %get-tuple-element.289, s32[8]{0:T(128)S(1)} %get-tuple-element.271, f32[8,256,1024]{2,1,0:T(8,128)} %fusion.29), kind=kCustom, calls=%fused_computation.2.clone.1 | custom fusion | flops 2097152 | bytes 25165856 | tf_op jit(solution)/shard_map/while/body/eval_jaxpr/scatter-add | solution.py:77
  350.8 5.4 copy.20
  357.3 68.2 %all-reduce = (f32[1024]{0:T(1024)S(1)}, f32[1024]{0:T(1024)S(1)}) all-reduce(f32[1024]{0:T(1024)S(1)} %dynamic_update_slice.6, f32[1024]{0:T(1024)S(1)} %dynamic_update_slice.7), channel_id=1, replica_groups=mesh['user'=16,'item'=8] {'user','item'}, use_global_device_ids=true, to_apply=%region_6.7 | all-reduce | flops 2048 | bytes 16384 | tf_op jit(solution)/shard_map/psum | solution.py:99
  425.5 32.8 %all-reduce.3.cloned.1.call-done = f32[2048,1024]{1,0:T(8,128)} async-done(((f32[2048,1024]{1,0:T(8,128)}), f32[2048,1024]{1,0:T(8,128)}) %all-reduce.3.cloned.1.call-update) | async-done | bytes 8388624 | tf_op jit(solution)/shard_map/psum | solution.py:101
  458.3 6.0 %divide_reduce_fusion = (f32[2048]{0:T(1024)S(1)}, f32[2048,1024]{1,0:T(8,128)S(1)}, f32[2048,1024]{1,0:T(8,128)S(1)}) fusion(f32[1024]{0:T(1024)S(1)} %get-tuple-element.190, f32[2048]{0:T(1024)S(1)} %broadcast_divide_fusion, f32[2048,1024]{1,0:T(8,128)} %all-reduce.3.cloned.1.call-done, bf16[2048,1024]{1,0:T(8,128)(2,1)} %bitcast.25), kind=kLoop, calls=%fused_computation.28 | loop fusion | flops 12580864 | bytes 29380608 | tf_op jit(solution)/shard_map/reduce_sum | solution.py:104
  464.9 1.6 dynamic-slice_log_fusion
  466.5 72.3 %reduce-scatter.2.cloned.1.call-done = f32[1024,64]{0,1:T(8,128)} async-done(((f32[1024,1024]{0,1:T(8,128)}), f32[1024,64]{0,1:T(8,128)}) %reduce-scatter.2.cloned.1.call-update) | async-done | bytes 262160 | tf_op jit(solution)/shard_map/reduce_scatter | solution.py:111
  538.8 1.8 fusion.23
  540.7 38.1 %psum.31 = f32[1024]{0:T(1024)S(1)} all-reduce(f32[1024]{0:T(1024)S(1)} %get-tuple-element.196), channel_id=1, replica_groups=mesh['user'=16,'item'=8] {'user'}, use_global_device_ids=true, to_apply=%region_12.13 | all-reduce | flops 1024 | bytes 8192 | tf_op jit(solution)/shard_map/psum | solution.py:117
  (56 shorter events, 3.6 us)
Async XLA Ops:
  7.2 52.1 %all-gather.5.cloned.1.call-start = ((), (), s32[]{:S(2)}) async-start(), calls=%async_computation.2 | async-start | bytes 2228224 | tf_op jit(solution)/shard_map/all_gather | solution.py:44
  11.4 85.5 %all-gather.3.cloned.1.call-start = ((), (), s32[]{:S(2)}) async-start(), calls=%async_computation.1 | async-start | bytes 4718592 | tf_op jit(solution)/shard_map/all_gather | solution.py:43
  21.3 437.0 %all-reduce.3.cloned.1.call-start = ((), (), s32[]{:S(2)}) async-start(), calls=%async_computation.3 | async-start | bytes 16777216 | tf_op jit(solution)/shard_map/psum | solution.py:101
  111.4 5.7 copy-start
  116.5 6.7 %copy-start.6 = (f32[8,256,256]{2,1,0:T(8,128)}, f32[8,256,256]{2,1,0:T(8,128)S(1)}, u32[]{:S(2)}) copy-start(f32[8,256,256]{2,1,0:T(8,128)S(1)} %fusion.28) | copy-start | bytes 6291460 | tf_op jit(solution)/shard_map/while
  173.0 5.8 copy-start
  178.0 6.7 %copy-start.6 = (f32[8,256,256]{2,1,0:T(8,128)}, f32[8,256,256]{2,1,0:T(8,128)S(1)}, u32[]{:S(2)}) copy-start(f32[8,256,256]{2,1,0:T(8,128)S(1)} %fusion.28) | copy-start | bytes 6291460 | tf_op jit(solution)/shard_map/while
  234.4 5.8 copy-start
  239.5 6.7 %copy-start.6 = (f32[8,256,256]{2,1,0:T(8,128)}, f32[8,256,256]{2,1,0:T(8,128)S(1)}, u32[]{:S(2)}) copy-start(f32[8,256,256]{2,1,0:T(8,128)S(1)} %fusion.28) | copy-start | bytes 6291460 | tf_op jit(solution)/shard_map/while
  296.7 5.8 copy-start
  301.8 6.7 %copy-start.6 = (f32[8,256,256]{2,1,0:T(8,128)}, f32[8,256,256]{2,1,0:T(8,128)S(1)}, u32[]{:S(2)}) copy-start(f32[8,256,256]{2,1,0:T(8,128)S(1)} %fusion.28) | copy-start | bytes 6291460 | tf_op jit(solution)/shard_map/while
  350.8 188.0 %reduce-scatter.2.cloned.1.call-start = ((), (), s32[]{:S(2)}) async-start(), calls=%async_computation.4 | async-start | bytes 4456448 | tf_op jit(solution)/shard_map/reduce_scatter | solution.py:111
  356.2 0.7 copy-start.5
  356.2 0.8 copy-start.4
  356.2 69.3 %copy-start.3 = (f32[1024]{0:T(1024)S(1)}, f32[1024]{0:T(1024)}, u32[]{:S(2)}) copy-start(f32[1024]{0:T(1024)} %param.16) | copy-start | bytes 12292
  356.2 69.3 %copy-start.2 = (f32[2048]{0:T(1024)S(1)}, f32[2048]{0:T(1024)}, u32[]{:S(2)}) copy-start(f32[2048]{0:T(1024)} %param.13) | copy-start | bytes 24580
  464.3 74.5 %copy-start.1 = (bf16[1024,64]{0,1:T(8,128)(2,1)S(1)}, bf16[1024,64]{0,1:T(8,128)(2,1)}, u32[]{:S(2)}) copy-start(bf16[1024,64]{0,1:T(8,128)(2,1)} %get-tuple-element.204) | copy-start | bytes 393220
Sparse Core Ops, SparseCore 0:
  11.5 47.7 all-gather.4
  61.5 35.2 all-gather.2
  350.9 107.3 all-reduce.2
  461.5 77.2 reduce-scatter.1
where the time goes:
time: 587 us; the launch traced here: 586 us
  waiting for transfers between devices  177 us (30%)
  other arithmetic  165 us (28%)
  blocking collectives  106 us (18%)
  matrix products  75 us (13%)
  local copies, waits for them, and re-layouts  48.5 us (8%)
  between operations  13.8 us (2%)
    reduce_scatter x1, waiting for transfers between devices, on_device(): lax.psum_scatter(item_acc, 'user', scatter_dimension=1, tiled=True)  72.3 us
    scatter-add x4, other arithmetic, group_step(): user_acc = user_acc.at[rows_user].add(user_terms)  69.2 us
    scatter-add x4, other arithmetic, group_step(): item_acc = item_acc.at[rows_item].add(item_terms)  68.9 us
    psum x1, blocking collectives, on_device(): lax.psum((beta_placed, theta_placed), ('user', 'item'))  68.2 us
    psum x1, blocking collectives, on_device(): eta_rate_new = prior_c2 / prior_d2 + lax.psum(item_part, 'user')  38.1 us
    all_gather x1, waiting for transfers between devices, on_device(): beta_full = lax.all_gather(beta_part, 'user', axis=1, tiled=True)  37.3 us
    all_gather x1, waiting for transfers between devices, on_device(): theta_full = lax.all_gather(theta_part, 'item', axis=1, tiled=True)  34.7 us
    psum x1, waiting for transfers between devices, on_device(): user_summed = lax.psum(user_acc, 'item')  32.8 us
  transfers between devices with their start and end apart: 4, of which 4 were waited for; matrix products, arithmetic and copies ran while one was open for 5% of the time, Pallas kernels for 0%

commit v1 on v0

v1 whole, which is shorter than its diff:
```python
import jax
import jax.numpy as jnp
from jax import lax
from jax.experimental import pallas as pl
from jax.experimental.pallas import tpu as pltpu
from jax.sharding import PartitionSpec as P

prior_a = 0.3
prior_a2 = 0.3
prior_b2 = 1.0
prior_c = 0.3
prior_c2 = 0.3
prior_d2 = 1.0

K = 1024
UB = 8
BLK = 256
TMAX = 32
F32 = jnp.float32
BF16 = jnp.bfloat16
MESH = pl.DeviceIdType.MESH
SLOTS = 17
FIRST = 6


def exp_mean_log(s, r):
    w = s * (s + 3.0)
    prod = w * (w + 2.0)
    y = s + 4.0
    yr = y * r
    inv = 1.0 / (prod * yr)
    inv_prod = inv * yr
    v = inv * prod * r
    inv_r = inv * prod * y
    rec = (2.0 * s + 3.0) * (2.0 * w + 2.0) * inv_prod
    v2 = v * v
    series = v2 * (1.0 / 12 - v2 * (1.0 / 120 - v2 * (1.0 / 252 - v2 * (1.0 / 240))))
    return y * jnp.exp(-(rec + 0.5 * v + series)) * inv_r, s * inv_r


def kernel(
    slots_ref,
    live_ref,
    th_s,
    th_r,
    be_s,
    be_r,
    counts,
    xi_ref,
    eta_ref,
    out_user,
    out_item,
    out_xi,
    out_eta,
    out_tot,
    th_s_v,
    th_r_v,
    be_s_v,
    be_r_v,
    counts_v,
    TF,
    BT,
    R,
    IT,
    UF,
    U16,
    UR,
    S1s,
    S1r,
    S2s,
    S2r,
    J1s,
    J1r,
    J2s,
    J2r,
    J3s,
    J3r,
    ou_v,
    TL,
    TS0,
    TS1,
    TS2,
    TR1,
    TR2,
    TR3,
    TTc,
    XIP,
    XR,
    EP0,
    EP1,
    ER1,
    ER2,
    lsem,
    osem,
    gS,
    gR,
    bS,
    bR,
    sS,
    sR,
    s1S,
    s1R,
    s2S,
    s2R,
    jS,
    jR,
    tS,
    tR,
    eS,
    eR,
):
    user = lax.axis_index("user")
    item = lax.axis_index("item")
    x, c = item // 2, item % 2
    y, z = user // 4, user % 4
    q, p = item, user

    def m4(v):
        return (v + 4) % 4

    def dev(dx=0, dc=0, dy=0, dz=0):
        return (m4(y + dy) * 4 + m4(z + dz), m4(x + dx) * 2 + (c + dc) % 2)

    item_peers = [(dx, dc) for dx in range(4) for dc in range(2) if dx or dc]

    bar = pltpu.get_barrier_semaphore()
    for dx, dc in item_peers:
        pl.semaphore_signal(bar, inc=1, device_id=dev(dx=dx, dc=dc), device_id_type=MESH)
    for d in (1, 2, 3):
        pl.semaphore_signal(bar, inc=1, device_id=dev(dy=d), device_id_type=MESH)
        pl.semaphore_signal(bar, inc=1, device_id=dev(dz=d), device_id_type=MESH)

    def load(u, k):
        src, dst = ((th_s, th_s_v), (th_r, th_r_v))[k]
        return pltpu.make_async_copy(
            src.at[pl.ds(pl.multiple_of(u * BLK, BLK), BLK), :], dst.at[u], lsem.at[2 * u + k]
        )

    be_loads = [
        pltpu.make_async_copy(be_s, be_s_v, lsem.at[16]),
        pltpu.make_async_copy(be_r, be_r_v, lsem.at[17]),
    ]
    counts_load = pltpu.make_async_copy(counts, counts_v, lsem.at[18])
    for d in be_loads:
        d.start()
    for u in range(UB):
        load(u, 0).start()
        load(u, 1).start()
    counts_load.start()

    def rc(src, dst, ss, rs, to):
        return pltpu.make_async_remote_copy(
            src_ref=src, dst_ref=dst, send_sem=ss, recv_sem=rs, device_id=to, device_id_type=MESH
        )

    def total_item(k, n):
        dx, dc = item_peers[n]
        return rc(TS0.at[k], TR1.at[k, q], tS.at[k, n], tR.at[k, n], dev(dx=dx, dc=dc))

    def total_z(k, d):
        return rc(TS1.at[k], TR2.at[k, z], tS.at[k, 6 + d], tR.at[k, 6 + d], dev(dz=d))

    def total_y(k, d):
        return rc(TS2.at[k], TR3.at[k, y], tS.at[k, 9 + d], tR.at[k, 9 + d], dev(dy=d))

    def total_1(k):
        TR1[k, q] = TS0[k]
        for n in range(7):
            total_item(k, n).start()

    def total_2(k):
        for n in range(7):
            total_item(k, n).wait()
        TS1[k] = jnp.sum(TR1[k], axis=0)
        TR2[k, z] = TS1[k]
        for d in (1, 2, 3):
            total_z(k, d).start()

    def total_3(k):
        for d in (1, 2, 3):
            total_z(k, d).wait()
        TS2[k] = jnp.sum(TR2[k], axis=0)
        TR3[k, y] = TS2[k]
        for d in (1, 2, 3):
            total_y(k, d).start()

    def total_4(k):
        for d in (1, 2, 3):
            total_y(k, d).wait()
        out_tot[k] = jnp.sum(TR3[k], axis=0)

    A, B = slice(0, 32), slice(32, 64)

    def b1(h, ab, d):
        rows = (A, B)[ab]
        ref = BT.at[h, y, z, rows, :]
        return rc(ref, ref, bS.at[h, ab, d - 1], bR.at[h, ab, d - 1], dev(dy=d) if ab == 0 else dev(dz=d))

    def b2(h, ab, n):
        step = (1, 3)[n]
        if ab == 0:
            ref, to = BT.at[h, :, z, A, :], dev(dz=step)
        else:
            ref, to = BT.at[h, y, :, B, :], dev(dy=step)
        return rc(ref, ref, bS.at[h, ab, 3 + n], bR.at[h, ab, 3 + n], to)

    def b3(h, ab, n):
        step, back = ((1, 3), (3, 1))[n]
        two = slice(0, 2) if n == 0 else slice(2, 4)
        if ab == 0:
            ref, to = BT.at[h, two, m4(z + back), A, :], dev(dz=step)
        else:
            ref, to = BT.at[h, m4(y + back), two, B, :], dev(dy=step)
        return rc(ref, ref, bS.at[h, ab, 5 + n], bR.at[h, ab, 5 + n], to)

    def beta_2(h):
        for ab in range(2):
            for d in (1, 2, 3):
                b1(h, ab, d).wait_recv()
            for n in range(2):
                b2(h, ab, n).start()

    def beta_3(h):
        for ab in range(2):
            for n in range(2):
                b2(h, ab, n).wait_recv()
            for n in range(2):
                b3(h, ab, n).start()

    def beta_4(h):
        for ab in range(2):
            for n in range(2):
                b3(h, ab, n).wait_recv()

    def g(u, n):
        sems = dict(ss=gS.at[u, n], rs=gR.at[u, n])
        q1, q3, q2 = m4(x + 1) * 2 + c, m4(x + 3) * 2 + c, m4(x + 2) * 2 + c
        ref, to = {
            0: (lambda: (TF.at[q, u], dev(dx=1))),
            1: (lambda: (TF.at[q, u], dev(dx=3))),
            2: (lambda: (TF.at[q, u], dev(dc=1))),
            3: (lambda: (TF.at[q3, u, pl.ds(0, 128), :], dev(dx=1))),
            4: (lambda: (TF.at[q1, u, pl.ds(128, 128), :], dev(dx=3))),
            5: (lambda: (TF.at[q3, u], dev(dc=1))),
            6: (lambda: (TF.at[q1, u], dev(dc=1))),
            7: (lambda: (TF.at[q2, u], dev(dc=1))),
        }[n]()
        return rc(ref, ref, sems["ss"], sems["rs"], to)

    def own(u):
        load(u, 0).wait()
        load(u, 1).wait()
        e, mean = exp_mean_log(th_s_v[u], th_r_v[u])
        TF[q, u] = e.astype(BF16)
        TL[...] += jnp.sum(mean.reshape(32, 8, 128), axis=0)
        for n in (0, 1, 2):
            g(u, n).start()

    def forward_1(u):
        g(u, 0).wait_recv()
        g(u, 3).start()
        g(u, 5).start()
        g(u, 1).wait_recv()
        g(u, 4).start()
        g(u, 6).start()

    def forward_2(u):
        g(u, 3).wait_recv()
        g(u, 4).wait_recv()
        g(u, 7).start()

    def gathered(u):
        for n in (2, 5, 6, 7):
            g(u, n).wait_recv()

    def tiles(u):
        gathered(u)
        t_blocks = [
            jnp.concatenate([TF[2 * kb, u], TF[2 * kb + 1, u]], axis=1) for kb in range(4)
        ]
        t_all = jnp.concatenate(t_blocks, axis=1)
        live = live_ref[0]
        for j in range(4):
            h, n = j // 2, j % 2
            cols = slice(n * 256, (n + 1) * 256)
            weights = BT[h, :, :, :, cols].reshape(K, 256)
            denominator = jnp.dot(t_all, weights, preferred_element_type=F32)
            pos = u * 4 + j
            slot = jnp.int32(0)
            for t in range(TMAX):
                slot = jnp.where(slots_ref[t] == pos, t, slot)
            mask = (slot < live).astype(F32)
            tile_counts = counts_v[slot].astype(F32) * mask
            R[h, :, cols] = (tile_counts / denominator).astype(BF16)
        r_blocks = [R[0], R[1]]
        x_col = []
        for r in range(2):
            row = (prior_a2 + K * prior_a) / xi_ref[pl.ds(2 * u + r, 1), :]
            x_col.append(jnp.broadcast_to(row, (128, 128)).T)
        xi_mean = jnp.concatenate(x_col, axis=0)
        acc = jnp.zeros((256, 128), F32)
        for kb in range(4):
            terms = None
            for h in range(2):
                part = lax.dot_general(
                    r_blocks[h],
                    BT[h, kb].reshape(256, 512),
                    (((1,), (1,)), ((), ())),
                    preferred_element_type=F32,
                )
                terms = part if terms is None else terms + part
            for half in range(2):
                k8 = 2 * kb + half
                block = terms[:, half * 128 : (half + 1) * 128]
                UF[u, k8] = block
                U16[u, k8 // 2, k8 % 2] = block.astype(BF16)
                t = t_blocks[kb][:, half * 128 : (half + 1) * 128].astype(F32)
                rate = xi_mean + out_tot[0, k8 : k8 + 1, :]
                acc = acc + (prior_a / 8 + t * block) / rate
        rows = [jnp.sum(acc[r * 128 : (r + 1) * 128].T, axis=0, keepdims=True) for r in range(2)]
        XIP[u] = jnp.concatenate(rows, axis=0)
        sib(u).start()
        for kb in range(4):
            t_t = t_blocks[kb].T
            for h in range(2):
                part = jnp.dot(t_t, r_blocks[h], preferred_element_type=F32)
                IT[h, kb] += part.reshape(4, 64, 512)

    def sib(u):
        return rc(U16.at[u, :, 1 - c], UR.at[u], sS.at[u], sR.at[u], dev(dc=1))

    def s1(u, n):
        rows = pl.ds(n * 128, 128)
        return rc(S1s.at[u, rows, :], S1r.at[u, rows, :], s1S.at[u, n], s1R.at[u, n], dev(dx=(1, 3)[n]))

    def s2(u, n):
        return rc(S2s.at[u, n], S2r.at[u, n], s2S.at[u, n], s2R.at[u, n], dev(dx=(1, 3)[n]))

    def reduce_1(u):
        sib(u).wait_recv()
        x2 = m4(x + 2)
        S1s[u] = (UF[u, 2 * x2 + c] + UR[u, x2].astype(F32)).astype(BF16)
        s1(u, 0).start()
        s1(u, 1).start()

    def reduce_2(u):
        for n in range(2):
            s1(u, n).wait_recv()
            xn = m4(x + (1, 3)[n])
            total = UF[u, 2 * xn + c] + UR[u, xn].astype(F32)
            got = S1r[u, pl.ds(n * 128, 128), :].astype(F32)
            mine, plain = total[n * 128 : (n + 1) * 128], total[(1 - n) * 128 : (2 - n) * 128]
            S2s[u, n, pl.ds(n * 128, 128), :] = (mine + got).astype(BF16)
            S2s[u, n, pl.ds((1 - n) * 128, 128), :] = plain.astype(BF16)
            s2(u, n).start()

    def write_user(u):
        return pltpu.make_async_copy(
            ou_v.at[u], out_user.at[pl.ds(pl.multiple_of(u * BLK, BLK), BLK), :], osem.at[u]
        )

    def reduce_3(u):
        s2(u, 0).wait_recv()
        s2(u, 1).wait_recv()
        total = UF[u, q] + UR[u, x].astype(F32) + S2r[u, 0].astype(F32) + S2r[u, 1].astype(F32)
        ou_v[u] = prior_a + TF[q, u].astype(F32) * total
        write_user(u).start()

    def blocks(ab, at):
        return (lambda h: IT[h, :, at, A, :]) if ab == 0 else (lambda h: IT[h, at, :, B, :])

    def along(ab, first):
        on_z = (ab == 0) == first
        return (z, lambda d: dev(dz=d)) if on_z else (y, lambda d: dev(dy=d))

    def j1(h, ab, n):
        _, to = along(ab, True)
        ref = pl.ds(2 * n, 2)
        return rc(J1s.at[h, ab, ref], J1r.at[h, ab, ref], jS.at[h, ab, n], jR.at[h, ab, n], to((1, 3)[n]))

    def j2(h, ab, n):
        _, to = along(ab, True)
        return rc(J2s.at[h, ab, n], J2r.at[h, ab, n], jS.at[h, ab, 2 + n], jR.at[h, ab, 2 + n], to((1, 3)[n]))

    def j3(h, ab, d):
        me, to = along(ab, False)
        return rc(
            J3s.at[h, ab, m4(me + d)], J3r.at[h, ab, d - 1], jS.at[h, ab, 3 + d], jR.at[h, ab, 3 + d], to(d)
        )

    def item_1(h):
        for ab in range(2):
            me, _ = along(ab, True)
            J1s[h, ab] = blocks(ab, m4(me + 2))(h).astype(BF16)
            for n in range(2):
                j1(h, ab, n).start()

    def item_2(h):
        for ab in range(2):
            me, _ = along(ab, True)
            for n in range(2):
                j1(h, ab, n).wait_recv()
                part = blocks(ab, m4(me + (1, 3)[n]))(h)
                two, rest = slice(2 * n, 2 * n + 2), slice(2 - 2 * n, 4 - 2 * n)
                J2s[h, ab, n, two] = (part[two] + J1r[h, ab, two].astype(F32)).astype(BF16)
                J2s[h, ab, n, rest] = part[rest].astype(BF16)
                j2(h, ab, n).start()

    def item_3(h):
        for ab in range(2):
            me, _ = along(ab, True)
            for n in range(2):
                j2(h, ab, n).wait_recv()
            total = blocks(ab, me)(h) + J2r[h, ab, 0].astype(F32) + J2r[h, ab, 1].astype(F32)
            J3s[h, ab] = total.astype(BF16)
            if ab == 0:
                IT[h, :, z, A, :] = total
            else:
                IT[h, y, :, B, :] = total
            for d in (1, 2, 3):
                j3(h, ab, d).start()

    def item_4(h):
        for ab in range(2):
            rows = (A, B)[ab]
            for d in (1, 2, 3):
                j3(h, ab, d).wait_recv()
            total = IT[h, y, z, rows, :] + jnp.sum(J3r[h, ab].astype(F32), axis=0)
            out_item[rows, h * 512 : (h + 1) * 512] = (
                prior_c + BT[h, y, z, rows, :].astype(F32) * total
            )

    def xi_send(n):
        dx, dc = item_peers[n]
        return rc(XIP, XR.at[q], eS.at[n], eR.at[n], dev(dx=dx, dc=dc))

    def xi_1():
        XR[q] = XIP[...]
        for n in range(7):
            xi_send(n).start()

    def xi_2():
        for n in range(7):
            xi_send(n).wait()
        out_xi[...] = prior_a2 / prior_b2 + jnp.sum(XR[...], axis=0)

    def eta_z(d):
        return rc(EP0, ER1.at[z], eS.at[6 + d], eR.at[6 + d], dev(dz=d))

    def eta_y(d):
        return rc(EP1, ER2.at[y], eS.at[9 + d], eR.at[9 + d], dev(dy=d))

    def eta_1():
        for k8 in range(8):
            row = out_tot[1, k8 : k8 + 1, :]
            TTc[k8] = jnp.broadcast_to(row, (128, 128)).T
        for h in range(2):
            em = jnp.concatenate(
                [(prior_c2 + K * prior_c) / eta_ref[h * 4 + r : h * 4 + r + 1, :] for r in range(4)], axis=1
            )

            def step(k16, acc):
                yy, zz = k16 // 4, k16 % 4
                tt = TTc[k16 // 2, pl.ds(pl.multiple_of((k16 % 2) * 64, 64), 64), :]
                rate = jnp.concatenate([tt] * 4, axis=1) + em
                val = (prior_c / 16 + BT[h, yy, zz].astype(F32) * IT[h, yy, zz]) / rate
                return acc + jnp.sum(val.reshape(8, 8, 512), axis=0)

            acc = lax.fori_loop(0, 16, step, jnp.zeros((8, 512), F32))
            EP0[h] = jnp.sum(acc, axis=0, keepdims=True)
        ER1[z] = EP0[...]
        for d in (1, 2, 3):
            eta_z(d).start()

    def eta_2():
        for d in (1, 2, 3):
            eta_z(d).wait()
        EP1[...] = jnp.sum(ER1[...], axis=0)
        ER2[y] = EP1[...]
        for d in (1, 2, 3):
            eta_y(d).start()

    def eta_3():
        for d in (1, 2, 3):
            eta_y(d).wait()
        out_eta[...] = prior_c2 / prior_d2 + jnp.sum(ER2[...], axis=0)

    for d in be_loads:
        d.wait()
    sums = jnp.zeros((64, 128), F32)
    for ib in range(8):
        rows = slice(ib * 128, (ib + 1) * 128)
        e, mean = exp_mean_log(be_s_v[rows, :].T, be_r_v[rows, :].T)
        BT[ib // 4, y, z, :, (ib % 4) * 128 : (ib % 4 + 1) * 128] = e.astype(BF16)
        sums = sums + mean
    row = jnp.sum(jnp.concatenate([sums, sums], axis=0).T, axis=0, keepdims=True)
    lane = lax.broadcasted_iota(jnp.int32, (8, 128), 1)
    sub = lax.broadcasted_iota(jnp.int32, (8, 128), 0)
    TS0[0] = jnp.where((sub == p // 2) & (lane // 64 == p % 2), jnp.broadcast_to(row, (8, 128)), 0.0)
    TL[...] = jnp.zeros_like(TL)
    pl.semaphore_wait(bar, 13)
    for h in range(2):
        for ab in range(2):
            for d in (1, 2, 3):
                b1(h, ab, d).start()
    total_1(0)
    IT[...] = jnp.zeros_like(IT)

    def slot_step(s, carry):
        def at(first, task):
            @pl.when((s >= first) & (s < first + UB))
            def _():
                task(s - first)

        def once(when, *tasks):
            @pl.when(s == when)
            def _():
                for task in tasks:
                    task()

        at(0, own)
        at(2, forward_1)
        at(3, forward_2)
        once(0, lambda: beta_2(0))
        once(1, lambda: beta_2(1), lambda: total_2(0))
        once(2, lambda: beta_3(0))
        once(3, lambda: beta_3(1), lambda: total_3(0))
        once(5, lambda: total_4(0), counts_load.wait)
        once(FIRST, lambda: beta_4(0), lambda: beta_4(1))
        at(FIRST, tiles)
        once(8, theta_total_1)
        once(9, lambda: total_2(1))
        once(10, lambda: total_3(1))
        once(11, lambda: total_4(1))
        once(FIRST + 7, lambda: item_1(0), lambda: item_1(1), xi_1)
        at(FIRST + 1, reduce_1)
        at(FIRST + 2, reduce_2)
        at(FIRST + 3, reduce_3)
        once(FIRST + 8, lambda: item_2(0), lambda: item_2(1), eta_1, xi_2)
        once(FIRST + 9, lambda: item_3(0), lambda: item_3(1), eta_2)
        once(FIRST + 10, lambda: item_4(0), lambda: item_4(1), eta_3)
        return carry

    def theta_total_1():
        local = jnp.sum(TL[...], axis=0, keepdims=True)
        TS0[1] = jnp.where(sub == q, jnp.broadcast_to(local, (8, 128)), 0.0)
        total_1(1)

    lax.fori_loop(0, SLOTS, slot_step, 0)

    def drain(u, carry):
        for n in range(8):
            g(u, n).wait_send()
        sib(u).wait_send()
        for n in range(2):
            s1(u, n).wait_send()
            s2(u, n).wait_send()
        write_user(u).wait()
        return carry

    lax.fori_loop(0, UB, drain, 0)
    for h in range(2):
        for ab in range(2):
            for d in (1, 2, 3):
                b1(h, ab, d).wait_send()
                j3(h, ab, d).wait_send()
            for n in range(2):
                b2(h, ab, n).wait_send()
                b3(h, ab, n).wait_send()
                j1(h, ab, n).wait_send()
                j2(h, ab, n).wait_send()


def on_device(theta_shape, theta_rate, xi_rate, beta_shape, beta_rate, eta_rate, tile_slots, tile_counts, live_tiles):
    user = lax.axis_index("user")
    item = lax.axis_index("item")
    smem = pl.BlockSpec(memory_space=pltpu.SMEM)
    vmem = pl.BlockSpec(memory_space=pltpu.VMEM)
    hbm = pl.BlockSpec(memory_space=pltpu.HBM)
    dma = pltpu.SemaphoreType.DMA
    V = pltpu.VMEM
    user_new, item_new, xi_new, eta_new, totals = pl.pallas_call(
        kernel,
        out_shape=(
            jax.ShapeDtypeStruct((2048, 128), F32),
            jax.ShapeDtypeStruct((64, 1024), F32),
            jax.ShapeDtypeStruct((8, 2, 128), F32),
            jax.ShapeDtypeStruct((2, 1, 512), F32),
            jax.ShapeDtypeStruct((2, 8, 128), F32),
        ),
        in_specs=[smem, smem, hbm, hbm, hbm, hbm, hbm, vmem, vmem],
        out_specs=(hbm, vmem, vmem, vmem, vmem),
        scratch_shapes=[
            V((8, 256, 128), F32),
            V((8, 256, 128), F32),
            V((1024, 64), F32),
            V((1024, 64), F32),
            V((32, 256, 256), BF16),
            V((8, 8, 256, 128), BF16),
            V((2, 4, 4, 64, 512), BF16),
            V((2, 256, 512), BF16),
            V((2, 4, 4, 64, 512), F32),
            V((8, 8, 256, 128), F32),
            V((8, 4, 2, 256, 128), BF16),
            V((8, 4, 256, 128), BF16),
            V((8, 256, 128), BF16),
            V((8, 256, 128), BF16),
            V((8, 2, 256, 128), BF16),
            V((8, 2, 256, 128), BF16),
            V((2, 2, 4, 32, 512), BF16),
            V((2, 2, 4, 32, 512), BF16),
            V((2, 2, 2, 4, 32, 512), BF16),
            V((2, 2, 2, 4, 32, 512), BF16),
            V((2, 2, 4, 32, 512), BF16),
            V((2, 2, 3, 32, 512), BF16),
            V((8, 256, 128), F32),
            V((8, 128), F32),
            V((2, 8, 128), F32),
            V((2, 8, 128), F32),
            V((2, 8, 128), F32),
            V((2, 8, 8, 128), F32),
            V((2, 4, 8, 128), F32),
            V((2, 4, 8, 128), F32),
            V((8, 128, 128), F32),
            V((8, 2, 128), F32),
            V((8, 8, 2, 128), F32),
            V((2, 1, 512), F32),
            V((2, 1, 512), F32),
            V((4, 2, 1, 512), F32),
            V((4, 2, 1, 512), F32),
            dma((19,)),
            dma((8,)),
            dma((8, 8)),
            dma((8, 8)),
            dma((2, 2, 7)),
            dma((2, 2, 7)),
            dma((8,)),
            dma((8,)),
            dma((8, 2)),
            dma((8, 2)),
            dma((8, 2)),
            dma((8, 2)),
            dma((2, 2, 7)),
            dma((2, 2, 7)),
            dma((2, 13)),
            dma((2, 13)),
            dma((13,)),
            dma((13,)),
        ],
        compiler_params=pltpu.CompilerParams(
            collective_id=0, has_side_effects=True, vmem_limit_bytes=58 * 2**20
        ),
        cost_estimate=pl.CostEstimate(flops=13 * 10**9, bytes_accessed=10 * 2**20, transcendentals=10**6),
        name="update",
    )(
        tile_slots.reshape(TMAX),
        live_tiles.reshape(1),
        theta_shape,
        theta_rate,
        beta_shape,
        beta_rate,
        tile_counts.reshape(TMAX, BLK, BLK),
        xi_rate.reshape(16, 128),
        eta_rate.reshape(8, 128),
    )
    beta_total, theta_total = totals[0].reshape(K), totals[1].reshape(K)
    beta_slice = lax.dynamic_slice_in_dim(beta_total, item * 128, 128, 0)
    theta_slice = lax.dynamic_slice_in_dim(theta_total, user * 64, 64, 0)
    xi_mean = (prior_a2 + K * prior_a) / xi_rate
    eta_mean = (prior_c2 + K * prior_c) / eta_rate
    return (
        user_new,
        jnp.log(xi_mean[:, None] + beta_slice[None, :]),
        xi_new.reshape(2048),
        item_new.T,
        jnp.log(eta_mean[:, None] + theta_slice[None, :]),
        eta_new.reshape(1024),
    )


def solution(mesh):
    in_specs = (
        P("user", "item"),
        P("user", "item"),
        P("user"),
        P("item", "user"),
        P("item", "user"),
        P("item"),
        P("user", "item", None),
        P("user", "item", None, None, None),
        P("user", "item"),
    )
    out_specs = (
        P("user", "item"),
        P("user", "item"),
        P("user"),
        P("item", "user"),
        P("item", "user"),
        P("item"),
    )
    return jax.shard_map(on_device, mesh=mesh, in_specs=in_specs, out_specs=out_specs, check_vma=False)
```

time: 587 us -> 91.3 us (0.16)
  waiting for transfers between devices: 177 us -> 0 us
  other arithmetic: 165 us -> 2.15 us
  blocking collectives: 106 us -> 0 us
  Pallas kernels: 0 us -> 76.2 us
  matrix products: 75 us -> 0 us
  local copies, waits for them, and re-layouts: 48.5 us -> 11.2 us
  between operations: 13.8 us -> 1.3 us
    scatter-add x8 -> x0, other arithmetic: 138 us -> none  [the longest x4 69.2 us: group_step(): user_acc = user_acc.at[rows_user].add(user_terms)]
    psum x2 -> x0, blocking collectives: 106 us -> none  [the longest x1 68.2 us: on_device(): lax.psum((beta_placed, theta_placed), ('user', 'item'))]
    pallas_call x0 -> x1, Pallas kernels: none -> 76.2 us  [on_device(): pl.pallas_call(kernel, out_shape=(jax.ShapeDtypeStruct((2048, 128), F32),...]
    dot_general x12 -> x0, matrix products: 75 us -> none  [the longest x4 30.8 us: group_step(): jnp.einsum('tui,tik->tuk', ratio_tile, items, preferred_element_type=jnp....]
    reduce_scatter x1 -> x0, waiting for transfers between devices: 72.3 us -> none  [on_device(): lax.psum_scatter(item_acc, 'user', scatter_dimension=1, tiled=True)]
    all_gather x2 -> x0, waiting for transfers between devices: 72 us -> none  [the longest x1 37.3 us: on_device(): beta_full = lax.all_gather(beta_part, 'user', axis=1, tiled=True)]
    psum x1 -> x0, waiting for transfers between devices: 32.8 us -> none  [on_device(): user_summed = lax.psum(user_acc, 'item')]
    gather x8 -> x0, local copies, waits for them, and re-layouts: 30.8 us -> none  [the longest x4 19.7 us: group_step(): users = jnp.take(theta_blocks, rows_user, axis=0)]
  transfers between devices with their start and end apart: 4 -> 0, of which waited for: 4 -> 0; matrix products, arithmetic and copies ran while one was open for 5% -> 0% of each run, Pallas kernels for 0% -> 0%
where the time goes in v1:
time: 91.3 us; the launch traced here: 90.9 us
  Pallas kernels  76.2 us (83%)
  local copies, waits for them, and re-layouts  11.2 us (12%)
  other arithmetic  2.15 us (2%)
  between operations  1.3 us (1%)
    pallas_call x1, Pallas kernels, on_device(): pl.pallas_call(kernel, out_shape=(jax.ShapeDtypeStruct((2048, 128), F32),...  76.2 us
    unnamed x10, local copies, waits for them, and re-layouts  10.4 us

profile of v1, /device:TPU:0, one launch (start us, length us, event | category | flops | bytes accessed | tf_op | source)
XLA Modules:
  0.0 90.9 jit_solution(1766700817411378136)
XLA Ops:
  1.3 1.9 %copy.15.be_s = f32[1024,64]{1,0:T(8,128)} copy(f32[1024,64]{0,1:T(8,128)} %param.12) | data formatting | bytes 524288 | tf_op args[3]
  3.2 1.9 %copy.16.be_r = f32[1024,64]{1,0:T(8,128)} copy(f32[1024,64]{0,1:T(8,128)} %param.13) | data formatting | bytes 524288 | tf_op args[4]
  5.2 0.0 copy-start
  5.2 0.0 copy-start.1
  5.2 76.2 %update.1 = (f32[2048,128]{1,0:T(8,128)}, f32[64,1024]{1,0:T(8,128)}, f32[8,2,128]{2,1,0:T(2,128)}, f32[2,1,512]{2,1,0:T(1,128)}, f32[2,8,128]{2,1,0:T(8,128)}) custom-call(s32[32]{0:T(128)} %bitcast.19, s32[1]{0:T(128)} %bitcast.12.live_ref, f32[2048,128]{1,0:T(8,128)} %th_s.1, f32[2048,128]{1,0:T(8,128)} %th_r.1, f32[1024,64]{1,0:T(8,128)} %copy.15.be_s, ...), custom_call_target="tpu_custom_call" | custom-call | flops 12999999488 | bytes 10485760 | tf_op jit(solution)/shard_map/update/pallas_call | solution.py:582
  81.4 0.7 slice_bitcast_fusion
  82.1 0.1 dynamic_slice.6
  82.1 0.0 copy-done
  82.1 1.3 %add_log_fusion = f32[2048,128]{1,0:T(8,128)} fusion(f32[128]{0:T(128)S(1)} %dynamic_slice.6, f32[2048]{0:T(1024)S(1)} %broadcast_divide_fusion), kind=kLoop, calls=%fused_computation | loop fusion | flops 262144 | bytes 1057280 | tf_op jit(solution)/shard_map/log | solution.py:673
  83.5 0.1 dynamic_slice.7
  83.5 0.0 copy-done.1
  83.5 0.8 add_log_fusion.1
  84.4 2.3 %copy.22 = f32[2048,128]{1,0:T(8,128)} copy(f32[2048,128]{1,0:T(8,128)} %get-tuple-element.24) | data formatting | bytes 2097152
  86.6 1.3 %copy.23 = f32[2048]{0:T(1024)} copy(f32[2048]{0:T(1024)} %bitcast.15) | data formatting | bytes 16384
  87.9 1.7 %copy.24 = f32[1024,64]{0,1:T(8,128)} copy(f32[1024,64]{0,1:T(8,128)} %bitcast.13) | data formatting | bytes 524288
  89.6 1.3 %copy.25 = f32[1024]{0:T(1024)} copy(f32[1024]{0:T(1024)} %bitcast.17) | data formatting | bytes 8192
  (2 shorter events, 0.0 us)
Async XLA Ops:
  5.2 77.0 %copy-start = (f32[2048]{0:T(1024)S(1)}, f32[2048]{0:T(1024)}, u32[]{:S(2)}) copy-start(f32[2048]{0:T(1024)} %param.11) | copy-start | bytes 24580
  5.2 78.4 %copy-start.1 = (f32[1024]{0:T(1024)S(1)}, f32[1024]{0:T(1024)}, u32[]{:S(2)}) copy-start(f32[1024]{0:T(1024)} %param.14) | copy-start | bytes 12292

commit v2 on v1

v2 whole, which is shorter than its diff:
```python
import jax
import jax.numpy as jnp
from jax import lax
from jax.experimental import pallas as pl
from jax.experimental.pallas import tpu as pltpu
from jax.sharding import PartitionSpec as P

prior_a = 0.3
prior_a2 = 0.3
prior_b2 = 1.0
prior_c = 0.3
prior_c2 = 0.3
prior_d2 = 1.0

K = 1024
UB = 8
BLK = 256
TMAX = 32
F32 = jnp.float32
BF16 = jnp.bfloat16
MESH = pl.DeviceIdType.MESH
OWN = [0, 1, 2, 3, 4, 5, 6, 7]
FORWARD_1 = [4, 5, 6, 7, 9, 10, 11, 12]
FORWARD_2 = [7, 9, 11, 12, 13, 14, 15, 16]
TILES = [13, 15, 17, 18]
FIRST_HALF = [19, 20, 21, 22]
SECOND_HALF = [23, 24, 25, 26]
REDUCE_1 = [16, 17, 18, 19, 25, 26, 27, 28]
REDUCE_2 = [18, 19, 21, 22, 28, 29, 30, 31]
REDUCE_3 = [21, 22, 24, 26, 31, 32, 33, 34]
BETA_2 = [4, 5]
BETA_3 = [8, 10]
BETA_4 = [13, 13]
ITEM_1 = [22, 26]
ITEM_2 = [26, 29]
ITEM_3 = [30, 32]
ITEM_4 = [33, 35]
ETA = [27, 32, 35]
XI = [26, 31]
TOTAL_BETA = [6, 8, 10]
TOTAL_THETA = [9, 13, 16, 19]
CLEAR = 3
SLOTS = 36


def exp_mean_log(s, r):
    w = s * (s + 3.0)
    prod = w * (w + 2.0)
    y = s + 4.0
    yr = y * r
    inv = 1.0 / (prod * yr)
    inv_prod = inv * yr
    v = inv * prod * r
    inv_r = inv * prod * y
    rec = (2.0 * s + 3.0) * (2.0 * w + 2.0) * inv_prod
    v2 = v * v
    series = v2 * (1.0 / 12 - v2 * (1.0 / 120 - v2 * (1.0 / 252 - v2 * (1.0 / 240))))
    return y * jnp.exp(-(rec + 0.5 * v + series)) * inv_r, s * inv_r


def kernel(
    slots_ref,
    live_ref,
    th_s,
    th_r,
    be_s,
    be_r,
    counts,
    xi_ref,
    eta_ref,
    out_user,
    out_item,
    out_xi,
    out_eta,
    out_tot,
    th_s_v,
    th_r_v,
    be_s_v,
    be_r_v,
    counts_v,
    TF,
    BT,
    R,
    IT,
    UF,
    U16,
    UR,
    S1s,
    S1r,
    S2s,
    S2r,
    J1s,
    J1r,
    J2s,
    J2r,
    J3s,
    J3r,
    TL,
    TS0,
    TS1,
    TS2,
    TR1,
    TR2,
    TR3,
    TTc,
    XIP,
    XR,
    EP0,
    EP1,
    ER1,
    ER2,
    lsem,
    gR,
    rR,
    jR,
    tR,
    send,
):
    user = lax.axis_index("user")
    item = lax.axis_index("item")
    x, c = item // 2, item % 2
    y, z = user // 4, user % 4
    q, p = item, user

    def m4(v):
        return (v + 4) % 4

    def dev(dx=0, dc=0, dy=0, dz=0):
        return (m4(y + dy) * 4 + m4(z + dz), m4(x + dx) * 2 + (c + dc) % 2)

    item_peers = [(dx, dc) for dx in range(4) for dc in range(2) if dx or dc]

    bar = pltpu.get_barrier_semaphore()
    for dx, dc in item_peers:
        pl.semaphore_signal(bar, inc=1, device_id=dev(dx=dx, dc=dc), device_id_type=MESH)
    for d in (1, 2, 3):
        pl.semaphore_signal(bar, inc=1, device_id=dev(dy=d), device_id_type=MESH)
        pl.semaphore_signal(bar, inc=1, device_id=dev(dz=d), device_id_type=MESH)

    be_loads = [
        pltpu.make_async_copy(be_s, be_s_v, lsem.at[0]),
        pltpu.make_async_copy(be_r, be_r_v, lsem.at[0]),
    ]
    first, later = pl.ds(0, BLK), pl.ds(BLK, 7 * BLK)
    th_loads = [
        pltpu.make_async_copy(th_s.at[first, :], th_s_v.at[first, :], lsem.at[1]),
        pltpu.make_async_copy(th_r.at[first, :], th_r_v.at[first, :], lsem.at[1]),
        pltpu.make_async_copy(th_s.at[later, :], th_s_v.at[later, :], lsem.at[2]),
        pltpu.make_async_copy(th_r.at[later, :], th_r_v.at[later, :], lsem.at[2]),
    ]
    counts_load = pltpu.make_async_copy(counts, counts_v, lsem.at[3])
    for d in be_loads + th_loads + [counts_load]:
        d.start()

    def landed(ref, sem):
        pltpu.make_async_copy(ref, ref, sem).wait()

    def rc(src, dst, ss, rs, to):
        return pltpu.make_async_remote_copy(
            src_ref=src, dst_ref=dst, send_sem=ss, recv_sem=rs, device_id=to, device_id_type=MESH
        )

    def total_item(k, n):
        dx, dc = item_peers[n]
        return rc(TS0.at[k], TR1.at[k, q], send.at[10], tR.at[3 * k], dev(dx=dx, dc=dc))

    def total_z(k, d):
        return rc(TS1.at[k], TR2.at[k, z], send.at[11], tR.at[3 * k + 1], dev(dz=d))

    def total_y(k, d):
        return rc(TS2.at[k], TR3.at[k, y], send.at[12], tR.at[3 * k + 2], dev(dy=d))

    def total_1(k):
        TR1[k, q] = TS0[k]
        for n in range(7):
            total_item(k, n).start()

    def total_2(k):
        landed(TR1.at[k, pl.ds(0, 7)], tR.at[3 * k])
        TS1[k] = jnp.sum(TR1[k], axis=0)
        TR2[k, z] = TS1[k]
        for d in (1, 2, 3):
            total_z(k, d).start()

    def total_3(k):
        landed(TR2.at[k, pl.ds(0, 3)], tR.at[3 * k + 1])
        TS2[k] = jnp.sum(TR2[k], axis=0)
        TR3[k, y] = TS2[k]
        for d in (1, 2, 3):
            total_y(k, d).start()

    def total_4(k):
        landed(TR3.at[k, pl.ds(0, 3)], tR.at[3 * k + 2])
        out_tot[k] = jnp.sum(TR3[k], axis=0)

    A, B = slice(0, 32), slice(32, 64)

    def b1(h, ab, d):
        rows = (A, B)[ab]
        ref = BT.at[h, y, z, rows, :]
        return rc(ref, ref, send.at[0], jR.at[0, h], dev(dy=d) if ab == 0 else dev(dz=d))

    def b2(h, ab, n):
        step = (1, 3)[n]
        if ab == 0:
            ref, to = BT.at[h, :, z, A, :], dev(dz=step)
        else:
            ref, to = BT.at[h, y, :, B, :], dev(dy=step)
        return rc(ref, ref, send.at[1], jR.at[1, h], to)

    def b3(h, ab, n):
        step, back = ((1, 3), (3, 1))[n]
        two = slice(0, 2) if n == 0 else slice(2, 4)
        if ab == 0:
            ref, to = BT.at[h, two, m4(z + back), A, :], dev(dz=step)
        else:
            ref, to = BT.at[h, m4(y + back), two, B, :], dev(dy=step)
        return rc(ref, ref, send.at[2], jR.at[2, h], to)

    def beta_2(h):
        landed(BT.at[h, pl.ds(0, 3), pl.ds(0, 2), A, :], jR.at[0, h])
        for ab in range(2):
            for n in range(2):
                b2(h, ab, n).start()

    def beta_3(h):
        landed(BT.at[h, pl.ds(0, 2)], jR.at[1, h])
        for ab in range(2):
            for n in range(2):
                b3(h, ab, n).start()

    def beta_4(h):
        landed(BT.at[h, 0], jR.at[2, h])

    def g(u, n):
        group = (0, 0, 2, 1, 1, 2, 2, 2)[n]
        q1, q3, q2 = m4(x + 1) * 2 + c, m4(x + 3) * 2 + c, m4(x + 2) * 2 + c
        ref, to = {
            0: (lambda: (TF.at[q, u], dev(dx=1))),
            1: (lambda: (TF.at[q, u], dev(dx=3))),
            2: (lambda: (TF.at[q, u], dev(dc=1))),
            3: (lambda: (TF.at[q3, u, pl.ds(0, 128), :], dev(dx=1))),
            4: (lambda: (TF.at[q1, u, pl.ds(128, 128), :], dev(dx=3))),
            5: (lambda: (TF.at[q3, u], dev(dc=1))),
            6: (lambda: (TF.at[q1, u], dev(dc=1))),
            7: (lambda: (TF.at[q2, u], dev(dc=1))),
        }[n]()
        return rc(ref, ref, send.at[3], gR.at[group, u], to)

    def own(u):
        @pl.when(u == 1)
        def _():
            th_loads[2].wait()
            th_loads[3].wait()

        rows = pl.ds(pl.multiple_of(u * BLK, BLK), BLK)
        e, mean = exp_mean_log(th_s_v[rows, :], th_r_v[rows, :])
        TF[q, u] = e.astype(BF16)
        TL[...] += jnp.sum(mean.reshape(32, 8, 128), axis=0)
        for n in (0, 1, 2):
            g(u, n).start()

    def forward_1(u):
        landed(TF.at[pl.ds(0, 2), u], gR.at[0, u])
        for n in (3, 5, 4, 6):
            g(u, n).start()

    def forward_2(u):
        landed(TF.at[0, u], gR.at[1, u])
        g(u, 7).start()

    def gathered(u):
        landed(TF.at[pl.ds(0, 4), u], gR.at[2, u])

    def user_block(u):
        return [jnp.concatenate([TF[2 * kb, u], TF[2 * kb + 1, u]], axis=1) for kb in range(4)]

    def ratios(u, h, t_all):
        live = live_ref[0, 0]
        for n in range(2):
            cols = slice(n * 256, (n + 1) * 256)
            weights = BT[h, :, :, :, cols].reshape(K, 256)
            denominator = jnp.dot(t_all, weights, preferred_element_type=F32)
            pos = u * 4 + h * 2 + n
            slot = jnp.int32(0)
            for t in range(TMAX):
                slot = jnp.where(slots_ref[t] == pos, t, slot)
            mask = (slot < live).astype(F32)
            tile_counts = counts_v[slot].astype(F32) * mask
            R[h, :, cols] = (tile_counts / denominator).astype(BF16)

    def user_terms(h, kb):
        return lax.dot_general(
            R[h], BT[h, kb].reshape(256, 512), (((1,), (1,)), ((), ())), preferred_element_type=F32
        )

    def item_terms(t_blocks, halves):
        for kb in range(4):
            t_t = t_blocks[kb].T
            for h in halves:
                part = jnp.dot(t_t, R[h], preferred_element_type=F32)
                IT[h, kb] += part.reshape(4, 64, 512)

    def finish(u, t_blocks, product):
        x_col = []
        for r in range(2):
            row = (prior_a2 + K * prior_a) / xi_ref[pl.ds(2 * u + r, 1), :]
            x_col.append(jnp.broadcast_to(row, (128, 128)).T)
        xi_mean = jnp.concatenate(x_col, axis=0)
        acc = jnp.zeros((256, 128), F32)
        for kb in range(4):
            terms = product(kb)
            for half in range(2):
                k8 = 2 * kb + half
                block = terms[half]
                UF[u, k8] = block
                U16[u, k8 // 2, k8 % 2] = block.astype(BF16)
                t = t_blocks[kb][:, half * 128 : (half + 1) * 128].astype(F32)
                rate = xi_mean + out_tot[0, k8 : k8 + 1, :]
                acc = acc + (prior_a / 8 + t * block) / rate
        rows = [jnp.sum(acc[r * 128 : (r + 1) * 128].T, axis=0, keepdims=True) for r in range(2)]
        XIP[u] = jnp.concatenate(rows, axis=0)
        sib(u).start()

    def tiles(u):
        gathered(u)
        t_blocks = user_block(u)
        t_all = jnp.concatenate(t_blocks, axis=1)
        ratios(u, 0, t_all)
        ratios(u, 1, t_all)

        def product(kb):
            terms = user_terms(0, kb) + user_terms(1, kb)
            return terms[:, :128], terms[:, 128:]

        finish(u, t_blocks, product)
        item_terms(t_blocks, (0, 1))

    def tiles_first(u):
        gathered(u)
        t_blocks = user_block(u)
        ratios(u, 0, jnp.concatenate(t_blocks, axis=1))
        for kb in range(4):
            terms = user_terms(0, kb)
            UF[u, 2 * kb] = terms[:, :128]
            UF[u, 2 * kb + 1] = terms[:, 128:]
        item_terms(t_blocks, (0,))

    def tiles_second(u):
        t_blocks = user_block(u)
        ratios(u, 1, jnp.concatenate(t_blocks, axis=1))

        def product(kb):
            terms = user_terms(1, kb)
            return UF[u, 2 * kb] + terms[:, :128], UF[u, 2 * kb + 1] + terms[:, 128:]

        finish(u, t_blocks, product)
        item_terms(t_blocks, (1,))

    def sib(u):
        return rc(U16.at[u, :, 1 - c], UR.at[u], send.at[4], rR.at[0, u], dev(dc=1))

    def s1(u, n):
        rows = pl.ds(n * 128, 128)
        return rc(S1s.at[u, rows, :], S1r.at[u, rows, :], send.at[5], rR.at[1, u], dev(dx=(1, 3)[n]))

    def s2(u, n):
        return rc(S2s.at[u, n], S2r.at[u, n], send.at[6], rR.at[2, u], dev(dx=(1, 3)[n]))

    def reduce_1(u):
        landed(UR.at[u], rR.at[0, u])
        x2 = m4(x + 2)
        S1s[u] = (UF[u, 2 * x2 + c] + UR[u, x2].astype(F32)).astype(BF16)
        s1(u, 0).start()
        s1(u, 1).start()

    def reduce_2(u):
        landed(S1r.at[u], rR.at[1, u])
        for n in range(2):
            xn = m4(x + (1, 3)[n])
            total = UF[u, 2 * xn + c] + UR[u, xn].astype(F32)
            got = S1r[u, pl.ds(n * 128, 128), :].astype(F32)
            mine, plain = total[n * 128 : (n + 1) * 128], total[(1 - n) * 128 : (2 - n) * 128]
            S2s[u, n, pl.ds(n * 128, 128), :] = (mine + got).astype(BF16)
            S2s[u, n, pl.ds((1 - n) * 128, 128), :] = plain.astype(BF16)
            s2(u, n).start()

    def reduce_3(u):
        landed(S2r.at[u], rR.at[2, u])
        total = UF[u, q] + UR[u, x].astype(F32) + S2r[u, 0].astype(F32) + S2r[u, 1].astype(F32)
        out_user[u] = prior_a + TF[q, u].astype(F32) * total

    def blocks(ab, at):
        return (lambda h: IT[h, :, at, A, :]) if ab == 0 else (lambda h: IT[h, at, :, B, :])

    def along(ab, first):
        on_z = (ab == 0) == first
        return (z, lambda d: dev(dz=d)) if on_z else (y, lambda d: dev(dy=d))

    def j1(h, ab, n):
        _, to = along(ab, True)
        ref = pl.ds(2 * n, 2)
        return rc(J1s.at[h, ab, ref], J1r.at[h, ab, ref], send.at[7], jR.at[3, h], to((1, 3)[n]))

    def j2(h, ab, n):
        _, to = along(ab, True)
        return rc(J2s.at[h, ab, n], J2r.at[h, ab, n], send.at[8], jR.at[4, h], to((1, 3)[n]))

    def j3(h, ab, d):
        me, to = along(ab, False)
        return rc(
            J3s.at[h, ab, m4(me + d)], J3r.at[h, ab, d - 1], send.at[9], jR.at[5, h], to(d)
        )

    def item_1(h):
        for ab in range(2):
            me, _ = along(ab, True)
            J1s[h, ab] = blocks(ab, m4(me + 2))(h).astype(BF16)
            for n in range(2):
                j1(h, ab, n).start()

    def item_2(h):
        landed(J1r.at[h], jR.at[3, h])
        for ab in range(2):
            me, _ = along(ab, True)
            for n in range(2):
                part = blocks(ab, m4(me + (1, 3)[n]))(h)
                two, rest = slice(2 * n, 2 * n + 2), slice(2 - 2 * n, 4 - 2 * n)
                J2s[h, ab, n, two] = (part[two] + J1r[h, ab, two].astype(F32)).astype(BF16)
                J2s[h, ab, n, rest] = part[rest].astype(BF16)
                j2(h, ab, n).start()

    def item_3(h):
        landed(J2r.at[h], jR.at[4, h])
        for ab in range(2):
            me, _ = along(ab, True)
            total = blocks(ab, me)(h) + J2r[h, ab, 0].astype(F32) + J2r[h, ab, 1].astype(F32)
            J3s[h, ab] = total.astype(BF16)
            if ab == 0:
                IT[h, :, z, A, :] = total
            else:
                IT[h, y, :, B, :] = total
            for d in (1, 2, 3):
                j3(h, ab, d).start()

    def item_4(h):
        landed(J3r.at[h], jR.at[5, h])
        for ab in range(2):
            rows = (A, B)[ab]
            total = IT[h, y, z, rows, :] + jnp.sum(J3r[h, ab].astype(F32), axis=0)
            out_item[rows, h * 512 : (h + 1) * 512] = (
                prior_c + BT[h, y, z, rows, :].astype(F32) * total
            )

    def xi_send(n):
        dx, dc = item_peers[n]
        return rc(XIP, XR.at[q], send.at[13], tR.at[6], dev(dx=dx, dc=dc))

    def xi_1():
        XR[q] = XIP[...]
        for n in range(7):
            xi_send(n).start()

    def xi_2():
        landed(XR.at[pl.ds(0, 7)], tR.at[6])
        out_xi[...] = prior_a2 / prior_b2 + jnp.sum(XR[...], axis=0)

    def eta_z(d):
        return rc(EP0, ER1.at[z], send.at[14], tR.at[7], dev(dz=d))

    def eta_y(d):
        return rc(EP1, ER2.at[y], send.at[15], tR.at[8], dev(dy=d))

    def eta_1():
        for k8 in range(8):
            row = out_tot[1, k8 : k8 + 1, :]
            TTc[k8] = jnp.broadcast_to(row, (128, 128)).T
        for h in range(2):
            em = jnp.concatenate(
                [(prior_c2 + K * prior_c) / eta_ref[h * 4 + r : h * 4 + r + 1, :] for r in range(4)], axis=1
            )

            def step(k16, acc):
                yy, zz = k16 // 4, k16 % 4
                tt = TTc[k16 // 2, pl.ds(pl.multiple_of((k16 % 2) * 64, 64), 64), :]
                rate = jnp.concatenate([tt] * 4, axis=1) + em
                val = (prior_c / 16 + BT[h, yy, zz].astype(F32) * IT[h, yy, zz]) / rate
                return acc + jnp.sum(val.reshape(8, 8, 512), axis=0)

            acc = lax.fori_loop(0, 16, step, jnp.zeros((8, 512), F32))
            EP0[h] = jnp.sum(acc, axis=0, keepdims=True)
        ER1[z] = EP0[...]
        for d in (1, 2, 3):
            eta_z(d).start()

    def eta_2():
        landed(ER1.at[pl.ds(0, 3)], tR.at[7])
        EP1[...] = jnp.sum(ER1[...], axis=0)
        ER2[y] = EP1[...]
        for d in (1, 2, 3):
            eta_y(d).start()

    def eta_3():
        landed(ER2.at[pl.ds(0, 3)], tR.at[8])
        out_eta[...] = prior_c2 / prior_d2 + jnp.sum(ER2[...], axis=0)

    for d in be_loads:
        d.wait()
    sums = jnp.zeros((64, 128), F32)
    for ib in range(8):
        rows = slice(ib * 128, (ib + 1) * 128)
        e, mean = exp_mean_log(be_s_v[:, rows], be_r_v[:, rows])
        BT[ib // 4, y, z, :, (ib % 4) * 128 : (ib % 4 + 1) * 128] = e.astype(BF16)
        sums = sums + mean
    row = jnp.sum(jnp.concatenate([sums, sums], axis=0).T, axis=0, keepdims=True)
    lane = lax.broadcasted_iota(jnp.int32, (8, 128), 1)
    sub = lax.broadcasted_iota(jnp.int32, (8, 128), 0)
    TS0[0] = jnp.where((sub == p // 2) & (lane // 64 == p % 2), jnp.broadcast_to(row, (8, 128)), 0.0)
    TL[...] = jnp.zeros_like(TL)
    out_tot[...] = jnp.zeros_like(out_tot)
    th_loads[0].wait()
    th_loads[1].wait()
    pl.semaphore_wait(bar, 13)
    for h in range(2):
        for ab in range(2):
            for d in (1, 2, 3):
                b1(h, ab, d).start()

    def theta_total_1():
        local = jnp.sum(TL[...], axis=0, keepdims=True)
        TS0[1] = jnp.where(sub == q, jnp.broadcast_to(local, (8, 128)), 0.0)
        total_1(1)

    def clear():
        IT[...] = jnp.zeros_like(IT)
        counts_load.wait()

    def slot_step(s, carry):
        def at(slots, task):
            here = s == slots[0]
            block = jnp.int32(0)
            for t in slots[1:]:
                here = here | (s == t)
                block = block + (s >= t).astype(jnp.int32)

            @pl.when(here)
            def _():
                task(block)

        def once(slots, tasks):
            for t, task in zip(slots, tasks):
                pl.when(s == t)(task)

        def halves(slots, task):
            for h, t in enumerate(slots):
                pl.when(s == t)(lambda h=h: task(h))

        at(OWN, own)
        at(FORWARD_1, forward_1)
        at(FORWARD_2, forward_2)
        once([0, CLEAR], [lambda: total_1(0), clear])
        halves(BETA_2, beta_2)
        halves(BETA_3, beta_3)
        halves(BETA_4, beta_4)
        once(TOTAL_BETA, [lambda: total_2(0), lambda: total_3(0), lambda: total_4(0)])
        at(REDUCE_2, reduce_2)
        at(REDUCE_1, reduce_1)
        at(TILES, tiles)
        at(FIRST_HALF, lambda n: tiles_first(n + 4))
        at(SECOND_HALF, lambda n: tiles_second(n + 4))
        once(TOTAL_THETA, [theta_total_1, lambda: total_2(1), lambda: total_3(1), lambda: total_4(1)])
        halves(ITEM_1, item_1)
        halves(ITEM_2, item_2)
        once([XI[0], ETA[0]], [xi_1, eta_1])
        halves(ITEM_3, item_3)
        halves(ITEM_4, item_4)
        at(REDUCE_3, reduce_3)
        once([XI[1]] + ETA[1:], [xi_2, eta_2, eta_3])
        return carry

    lax.fori_loop(0, SLOTS, slot_step, 0)

    landed(BT.at[0, pl.ds(0, 3), :, A, :], send.at[0])
    landed(BT.at[0], send.at[1])
    landed(BT.at[0, pl.ds(0, 2)], send.at[2])
    landed(TF.at[pl.ds(0, 7)], send.at[3])
    landed(UR, send.at[4])
    landed(S1s, send.at[5])
    landed(S2s, send.at[6])
    landed(J1s, send.at[7])
    landed(J2s, send.at[8])
    landed(J3r, send.at[9])
    landed(TR1.at[:, pl.ds(0, 7)], send.at[10])
    landed(TR2.at[:, pl.ds(0, 3)], send.at[11])
    landed(TR3.at[:, pl.ds(0, 3)], send.at[12])
    landed(XR.at[pl.ds(0, 7)], send.at[13])
    landed(ER1.at[pl.ds(0, 3)], send.at[14])
    landed(ER2.at[pl.ds(0, 3)], send.at[15])


def write_out(
    user_new, item_new, xi_new, eta_new, totals, xi_ref, eta_ref, o_user, o_ulog, o_xi, o_item, o_ilog, o_eta, ulog, tt, sem
):
    user = lax.axis_index("user")
    item = lax.axis_index("item")
    copy_user = pltpu.make_async_copy(user_new, o_user, sem.at[0])
    copy_user.start()
    beta_total = totals[0, pl.ds(item, 1), :]
    for u in range(UB):
        for r in range(2):
            row = (prior_a2 + K * prior_a) / xi_ref[2 * u + r : 2 * u + r + 1, :]
            col = jnp.broadcast_to(row, (128, 128)).T
            ulog[u, r * 128 : (r + 1) * 128, :] = jnp.log(col + beta_total)
        pltpu.make_async_copy(ulog.at[u], o_ulog.at[u], sem.at[1]).start()
    tt[...] = jnp.broadcast_to(totals[1, pl.ds(user // 2, 1), :], (128, 128)).T
    theta_total = tt[pl.ds(pl.multiple_of((user % 2) * 64, 64), 64), :]
    for ib in range(8):
        row = (prior_c2 + K * prior_c) / eta_ref[ib : ib + 1, :]
        o_ilog[:, ib * 128 : (ib + 1) * 128] = jnp.log(theta_total + row)
    o_item[...] = item_new[...]
    o_xi[...] = xi_new[...]
    o_eta[...] = eta_new[...]
    copy_user.wait()
    pltpu.make_async_copy(ulog, o_ulog, sem.at[1]).wait()


def on_device(theta_shape, theta_rate, xi_rate, beta_shape, beta_rate, eta_rate, tile_slots, tile_counts, live_tiles):
    xi_rows, eta_rows = xi_rate.reshape(16, 128), eta_rate.reshape(8, 128)
    smem = pl.BlockSpec(memory_space=pltpu.SMEM)
    vmem = pl.BlockSpec(memory_space=pltpu.VMEM)
    hbm = pl.BlockSpec(memory_space=pltpu.HBM)
    dma = pltpu.SemaphoreType.DMA
    V = pltpu.VMEM
    user_new, item_new, xi_new, eta_new, totals = pl.pallas_call(
        kernel,
        out_shape=(
            V((8, 256, 128), F32),
            V((64, 1024), F32),
            V((8, 2, 128), F32),
            V((2, 1, 512), F32),
            V((2, 8, 128), F32),
        ),
        in_specs=[smem, smem, hbm, hbm, hbm, hbm, hbm, vmem, vmem],
        out_specs=(vmem,) * 5,
        scratch_shapes=[
            V((2048, 128), F32),
            V((2048, 128), F32),
            V((64, 1024), F32),
            V((64, 1024), F32),
            V((32, 256, 256), BF16),
            V((8, 8, 256, 128), BF16),
            V((2, 4, 4, 64, 512), BF16),
            V((2, 256, 512), BF16),
            V((2, 4, 4, 64, 512), F32),
            V((8, 8, 256, 128), F32),
            V((8, 4, 2, 256, 128), BF16),
            V((8, 4, 256, 128), BF16),
            V((8, 256, 128), BF16),
            V((8, 256, 128), BF16),
            V((8, 2, 256, 128), BF16),
            V((8, 2, 256, 128), BF16),
            V((2, 2, 4, 32, 512), BF16),
            V((2, 2, 4, 32, 512), BF16),
            V((2, 2, 2, 4, 32, 512), BF16),
            V((2, 2, 2, 4, 32, 512), BF16),
            V((2, 2, 4, 32, 512), BF16),
            V((2, 2, 3, 32, 512), BF16),
            V((8, 128), F32),
            V((2, 8, 128), F32),
            V((2, 8, 128), F32),
            V((2, 8, 128), F32),
            V((2, 8, 8, 128), F32),
            V((2, 4, 8, 128), F32),
            V((2, 4, 8, 128), F32),
            V((8, 128, 128), F32),
            V((8, 2, 128), F32),
            V((8, 8, 2, 128), F32),
            V((2, 1, 512), F32),
            V((2, 1, 512), F32),
            V((4, 2, 1, 512), F32),
            V((4, 2, 1, 512), F32),
                dma((4,)),
            dma((3, 8)),
            dma((3, 8)),
            dma((6, 2)),
            dma((9,)),
            dma((16,)),
        ],
        compiler_params=pltpu.CompilerParams(
            collective_id=0, has_side_effects=True, vmem_limit_bytes=58 * 2**20
        ),
        cost_estimate=pl.CostEstimate(flops=13 * 10**9, bytes_accessed=10 * 2**20, transcendentals=10**6),
        name="update",
    )(
        tile_slots.reshape(TMAX),
        live_tiles,
        theta_shape,
        theta_rate,
        beta_shape.T,
        beta_rate.T,
        tile_counts.reshape(TMAX, BLK, BLK),
        xi_rows,
        eta_rows,
    )
    out = jax.ShapeDtypeStruct
    o_user, o_ulog, o_xi, o_item, o_ilog, o_eta = pl.pallas_call(
        write_out,
        out_shape=(
            out((8, 256, 128), F32),
            out((8, 256, 128), F32),
            out((8, 2, 128), F32),
            out((64, 1024), F32),
            out((64, 1024), F32),
            out((2, 1, 512), F32),
        ),
        in_specs=[vmem] * 7,
        out_specs=(hbm, hbm, vmem, vmem, vmem, vmem),
        scratch_shapes=[V((8, 256, 128), F32), V((128, 128), F32), dma((2,))],
        compiler_params=pltpu.CompilerParams(vmem_limit_bytes=16 * 2**20),
        name="write_out",
    )(user_new, item_new, xi_new, eta_new, totals, xi_rows, eta_rows)
    return (
        o_user.reshape(2048, 128),
        o_ulog.reshape(2048, 128),
        o_xi.reshape(2048),
        o_item.T,
        o_ilog.T,
        o_eta.reshape(1024),
    )


def solution(mesh):
    in_specs = (
        P("user", "item"),
        P("user", "item"),
        P("user"),
        P("item", "user"),
        P("item", "user"),
        P("item"),
        P("user", "item", None),
        P("user", "item", None, None, None),
        P("user", "item"),
    )
    out_specs = (
        P("user", "item"),
        P("user", "item"),
        P("user"),
        P("item", "user"),
        P("item", "user"),
        P("item"),
    )
    return jax.shard_map(on_device, mesh=mesh, in_specs=in_specs, out_specs=out_specs, check_vma=False)
```

time: 91.3 us -> 70.3 us (0.77)
  local copies, waits for them, and re-layouts: 11.2 us -> 0.01 us
  Pallas kernels: 76.2 us -> 68.8 us
  other arithmetic: 2.15 us -> 0 us
    unnamed x10 -> x4, local copies, waits for them, and re-layouts: 10.4 us -> 0.01 us
    pallas_call x1 -> x2, Pallas kernels: 76.2 us -> 68.8 us  [the longest x1 66.7 us: on_device(): pl.pallas_call(kernel, out_shape=(V((8, 256, 128), F32), V((64, 1024), F3...]
    log x2 -> x0, other arithmetic: 2.14 us -> none  [the longest x1 1.32 us: on_device(): jnp.log(xi_mean[:, None] + beta_slice[None, :])]
where the time goes in v2:
time: 70.3 us; the launch traced here: 70.1 us
  Pallas kernels  68.8 us (98%)
  between operations  1.32 us (2%)
    pallas_call x1, Pallas kernels, on_device(): pl.pallas_call(kernel, out_shape=(V((8, 256, 128), F32), V((64, 1024), F3...  66.7 us
    pallas_call x1, Pallas kernels, on_device(): pl.pallas_call(write_out, out_shape=(out((8, 256, 128), F32), out((8, 256...  2.11 us

profile of v2, /device:TPU:0, one launch (start us, length us, event | category | flops | bytes accessed | tf_op | source)
XLA Modules:
  0.0 70.1 jit_solution(13815814154135456527)
XLA Ops:
  1.3 0.0 copy-start
  1.3 0.0 copy-start.1
  1.3 66.7 %update.1 = (f32[8,256,128]{2,1,0:T(8,128)S(1)}, f32[64,1024]{1,0:T(8,128)S(1)}, f32[8,2,128]{2,1,0:T(2,128)S(1)}, f32[2,1,512]{2,1,0:T(1,128)S(1)}, f32[2,8,128]{2,1,0:T(8,128)S(1)}) custom-call(s32[32]{0:T(128)} %bitcast.25, s32[1,1]{1,0:T(1,128)S(6)} %copy.15.live_ref, f32[2048,128]{1,0:T(8,128)} %th_s.1, f32[2048,128]{1,0:T(8,128)} %th_r.1, ...), custom_call_target="tpu_custom_call" | custom-call | flops 12999999488 | bytes 10485760 | tf_op jit(solution)/shard_map/update/pallas_call | solution.py:634
  68.0 0.0 copy-done
  68.0 0.0 copy-done.1
  68.0 2.1 %write_out.1 = (f32[8,256,128]{2,1,0:T(8,128)}, f32[8,256,128]{2,1,0:T(8,128)}, f32[8,2,128]{2,1,0:T(2,128)}, f32[64,1024]{1,0:T(8,128)}, f32[64,1024]{1,0:T(8,128)}, /*index=5*/f32[2,1,512]{2,1,0:T(1,128)}) custom-call(f32[8,256,128]{2,1,0:T(8,128)S(1)} %get-tuple-element.17.user_new, f32[64,1024]{1,0:T(8,128)S(1)} %get-tuple-element.18.item_new, ...), custom_call_target="tpu_custom_call" | custom-call | tf_op jit(solution)/shard_map/write_out/pallas_call | solution.py:706
Async XLA Ops:
  1.3 66.7 %copy-start = (f32[2048]{0:T(1024)S(1)}, f32[2048]{0:T(1024)}, u32[]{:S(2)}) copy-start(f32[2048]{0:T(1024)} %param.11) | copy-start | bytes 24580
  1.3 66.7 %copy-start.1 = (f32[1024]{0:T(1024)S(1)}, f32[1024]{0:T(1024)}, u32[]{:S(2)}) copy-start(f32[1024]{0:T(1024)} %param.14) | copy-start | bytes 12292

commit v3 on v2

--- a/solution.py
+++ b/solution.py
@@ -19,26 +19,26 @@
 F32 = jnp.float32
 BF16 = jnp.bfloat16
 MESH = pl.DeviceIdType.MESH
-OWN = [0, 1, 2, 3, 4, 5, 6, 7]
-FORWARD_1 = [4, 5, 6, 7, 9, 10, 11, 12]
-FORWARD_2 = [7, 9, 11, 12, 13, 14, 15, 16]
-TILES = [13, 15, 17, 18]
-FIRST_HALF = [19, 20, 21, 22]
-SECOND_HALF = [23, 24, 25, 26]
-REDUCE_1 = [16, 17, 18, 19, 25, 26, 27, 28]
-REDUCE_2 = [18, 19, 21, 22, 28, 29, 30, 31]
-REDUCE_3 = [21, 22, 24, 26, 31, 32, 33, 34]
+OWN = [0, 1, 2, 4, 5, 6, 7, 9]
+FORWARD_1 = [4, 5, 6, 7, 9, 11, 12, 14]
+FORWARD_2 = [7, 9, 11, 12, 14, 15, 16, 17]
+TILES = [13, 14, 15, 16]
+FIRST_HALF = [17, 19]
+SECOND_HALF = [21, 22, 23, 24]
+REDUCE_1 = [15, 16, 17, 19, 24, 25, 26, 27]
+REDUCE_2 = [17, 19, 21, 22, 27, 28, 29, 30]
+REDUCE_3 = [21, 23, 25, 26, 31, 32, 33, 34]
 BETA_2 = [4, 5]
 BETA_3 = [8, 10]
 BETA_4 = [13, 13]
-ITEM_1 = [22, 26]
-ITEM_2 = [26, 29]
+ITEM_1 = [19, 24]
+ITEM_2 = [24, 28]
 ITEM_3 = [30, 32]
 ITEM_4 = [33, 35]
-ETA = [27, 32, 35]
-XI = [26, 31]
-TOTAL_BETA = [6, 8, 10]
-TOTAL_THETA = [9, 13, 16, 19]
+ETA = [26, 29, 31, 34]
+XI = [25, 32]
+TOTAL_BETA = [6, 8, 12]
+TOTAL_THETA = [10, 14, 16, 19]
 CLEAR = 3
 SLOTS = 36
 
@@ -272,33 +272,39 @@
     def gathered(u):
         landed(TF.at[pl.ds(0, 4), u], gR.at[2, u])
 
-    def user_block(u):
-        return [jnp.concatenate([TF[2 * kb, u], TF[2 * kb + 1, u]], axis=1) for kb in range(4)]
-
-    def ratios(u, h, t_all):
+    def factors(u, w):
+        blocks = pl.ds(u, w)
+        return [
+            jnp.concatenate([TF[2 * kb + i, blocks].reshape(w * 256, 128) for i in range(2)], axis=1)
+            for kb in range(4)
+        ]
+
+    def ratios(u, w, h, t_all):
         live = live_ref[0, 0]
         for n in range(2):
             cols = slice(n * 256, (n + 1) * 256)
             weights = BT[h, :, :, :, cols].reshape(K, 256)
             denominator = jnp.dot(t_all, weights, preferred_element_type=F32)
-            pos = u * 4 + h * 2 + n
-            slot = jnp.int32(0)
-            for t in range(TMAX):
-                slot = jnp.where(slots_ref[t] == pos, t, slot)
-            mask = (slot < live).astype(F32)
-            tile_counts = counts_v[slot].astype(F32) * mask
-            R[h, :, cols] = (tile_counts / denominator).astype(BF16)
-
-    def user_terms(h, kb):
-        return lax.dot_general(
-            R[h], BT[h, kb].reshape(256, 512), (((1,), (1,)), ((), ())), preferred_element_type=F32
-        )
-
-    def item_terms(t_blocks, halves):
+            for i in range(w):
+                rows = slice(i * 256, (i + 1) * 256)
+                pos = (u + i) * 4 + h * 2 + n
+                slot = jnp.int32(0)
+                for t in range(TMAX):
+                    slot = jnp.where(slots_ref[t] == pos, t, slot)
+                mask = (slot < live).astype(F32)
+                tile_counts = counts_v[slot].astype(F32) * mask
+                R[rows, h * 512 + n * 256 : h * 512 + (n + 1) * 256] = (tile_counts / denominator[rows]).astype(BF16)
+
+    def user_terms(w, halves, kb):
+        weights = jnp.concatenate([BT[h, kb].reshape(256, 512) for h in halves], axis=1)
+        ratio = R[: w * 256, halves[0] * 512 : halves[-1] * 512 + 512]
+        return lax.dot_general(ratio, weights, (((1,), (1,)), ((), ())), preferred_element_type=F32)
+
+    def item_terms(w, t_blocks, halves):
         for kb in range(4):
             t_t = t_blocks[kb].T
             for h in halves:
-                part = jnp.dot(t_t, R[h], preferred_element_type=F32)
+                part = jnp.dot(t_t, R[: w * 256, h * 512 : (h + 1) * 512], preferred_element_type=F32)
                 IT[h, kb] += part.reshape(4, 64, 512)
 
     def finish(u, t_blocks, product):
@@ -311,51 +317,49 @@
         for kb in range(4):
             terms = product(kb)
             for half in range(2):
-                k8 = 2 * kb + half
-                block = terms[half]
+                k8, cols = 2 * kb + half, slice(half * 128, (half + 1) * 128)
+                block = terms[:, cols]
                 UF[u, k8] = block
                 U16[u, k8 // 2, k8 % 2] = block.astype(BF16)
-                t = t_blocks[kb][:, half * 128 : (half + 1) * 128].astype(F32)
                 rate = xi_mean + out_tot[0, k8 : k8 + 1, :]
-                acc = acc + (prior_a / 8 + t * block) / rate
+                acc = acc + (prior_a / 8 + t_blocks[kb][:, cols].astype(F32) * block) / rate
         rows = [jnp.sum(acc[r * 128 : (r + 1) * 128].T, axis=0, keepdims=True) for r in range(2)]
         XIP[u] = jnp.concatenate(rows, axis=0)
         sib(u).start()
 
     def tiles(u):
         gathered(u)
-        t_blocks = user_block(u)
+        t_blocks = factors(u, 1)
         t_all = jnp.concatenate(t_blocks, axis=1)
-        ratios(u, 0, t_all)
-        ratios(u, 1, t_all)
+        ratios(u, 1, 0, t_all)
+        ratios(u, 1, 1, t_all)
+        finish(u, t_blocks, lambda kb: user_terms(1, (0, 1), kb))
+        item_terms(1, t_blocks, (0, 1))
+
+    def tiles_first(n):
+        u, w = 4 + 2 * n, 2
+        for i in range(w):
+            gathered(u + i)
+        t_blocks = factors(u, w)
+        ratios(u, w, 0, jnp.concatenate(t_blocks, axis=1))
+        for kb in range(4):
+            terms = user_terms(w, (0,), kb)
+            for i in range(w):
+                UF[u + i, 2 * kb] = terms[i * 256 : (i + 1) * 256, :128]
+                UF[u + i, 2 * kb + 1] = terms[i * 256 : (i + 1) * 256, 128:]
+        item_terms(w, t_blocks, (0,))
+
+    def tiles_second(n):
+        u = 4 + n
+        t_blocks = factors(u, 1)
+        ratios(u, 1, 1, jnp.concatenate(t_blocks, axis=1))
 
         def product(kb):
-            terms = user_terms(0, kb) + user_terms(1, kb)
-            return terms[:, :128], terms[:, 128:]
+            before = jnp.concatenate([UF[u, 2 * kb], UF[u, 2 * kb + 1]], axis=1)
+            return before + user_terms(1, (1,), kb)
 
         finish(u, t_blocks, product)
-        item_terms(t_blocks, (0, 1))
-
-    def tiles_first(u):
-        gathered(u)
-        t_blocks = user_block(u)
-        ratios(u, 0, jnp.concatenate(t_blocks, axis=1))
-        for kb in range(4):
-            terms = user_terms(0, kb)
-            UF[u, 2 * kb] = terms[:, :128]
-            UF[u, 2 * kb + 1] = terms[:, 128:]
-        item_terms(t_blocks, (0,))
-
-    def tiles_second(u):
-        t_blocks = user_block(u)
-        ratios(u, 1, jnp.concatenate(t_blocks, axis=1))
-
-        def product(kb):
-            terms = user_terms(1, kb)
-            return UF[u, 2 * kb] + terms[:, :128], UF[u, 2 * kb + 1] + terms[:, 128:]
-
-        finish(u, t_blocks, product)
-        item_terms(t_blocks, (1,))
+        item_terms(1, t_blocks, (1,))
 
     def sib(u):
         return rc(U16.at[u, :, 1 - c], UR.at[u], send.at[4], rR.at[0, u], dev(dc=1))
@@ -471,27 +475,28 @@
     def eta_y(d):
         return rc(EP1, ER2.at[y], send.at[15], tR.at[8], dev(dy=d))
 
-    def eta_1():
-        for k8 in range(8):
-            row = out_tot[1, k8 : k8 + 1, :]
-            TTc[k8] = jnp.broadcast_to(row, (128, 128)).T
-        for h in range(2):
-            em = jnp.concatenate(
-                [(prior_c2 + K * prior_c) / eta_ref[h * 4 + r : h * 4 + r + 1, :] for r in range(4)], axis=1
-            )
-
-            def step(k16, acc):
-                yy, zz = k16 // 4, k16 % 4
-                tt = TTc[k16 // 2, pl.ds(pl.multiple_of((k16 % 2) * 64, 64), 64), :]
-                rate = jnp.concatenate([tt] * 4, axis=1) + em
-                val = (prior_c / 16 + BT[h, yy, zz].astype(F32) * IT[h, yy, zz]) / rate
-                return acc + jnp.sum(val.reshape(8, 8, 512), axis=0)
-
-            acc = lax.fori_loop(0, 16, step, jnp.zeros((8, 512), F32))
-            EP0[h] = jnp.sum(acc, axis=0, keepdims=True)
-        ER1[z] = EP0[...]
-        for d in (1, 2, 3):
-            eta_z(d).start()
+    def eta_1(h):
+        if h == 0:
+            for k8 in range(8):
+                row = out_tot[1, k8 : k8 + 1, :]
+                TTc[k8] = jnp.broadcast_to(row, (128, 128)).T
+        em = jnp.concatenate(
+            [(prior_c2 + K * prior_c) / eta_ref[h * 4 + r : h * 4 + r + 1, :] for r in range(4)], axis=1
+        )
+
+        def step(k16, acc):
+            yy, zz = k16 // 4, k16 % 4
+            tt = TTc[k16 // 2, pl.ds(pl.multiple_of((k16 % 2) * 64, 64), 64), :]
+            rate = jnp.concatenate([tt] * 4, axis=1) + em
+            val = (prior_c / 16 + BT[h, yy, zz].astype(F32) * IT[h, yy, zz]) / rate
+            return acc + jnp.sum(val.reshape(8, 8, 512), axis=0)
+
+        acc = lax.fori_loop(0, 16, step, jnp.zeros((8, 512), F32))
+        EP0[h] = jnp.sum(acc, axis=0, keepdims=True)
+        if h == 1:
+            ER1[z] = EP0[...]
+            for d in (1, 2, 3):
+                eta_z(d).start()
 
     def eta_2():
         landed(ER1.at[pl.ds(0, 3)], tR.at[7])
@@ -555,9 +560,9 @@
             for h, t in enumerate(slots):
                 pl.when(s == t)(lambda h=h: task(h))
 
+        at(FORWARD_2, forward_2)
+        at(FORWARD_1, forward_1)
         at(OWN, own)
-        at(FORWARD_1, forward_1)
-        at(FORWARD_2, forward_2)
         once([0, CLEAR], [lambda: total_1(0), clear])
         halves(BETA_2, beta_2)
         halves(BETA_3, beta_3)
@@ -566,16 +571,17 @@
         at(REDUCE_2, reduce_2)
         at(REDUCE_1, reduce_1)
         at(TILES, tiles)
-        at(FIRST_HALF, lambda n: tiles_first(n + 4))
-        at(SECOND_HALF, lambda n: tiles_second(n + 4))
+        at(FIRST_HALF, tiles_first)
+        at(SECOND_HALF, tiles_second)
         once(TOTAL_THETA, [theta_total_1, lambda: total_2(1), lambda: total_3(1), lambda: total_4(1)])
         halves(ITEM_1, item_1)
         halves(ITEM_2, item_2)
-        once([XI[0], ETA[0]], [xi_1, eta_1])
+        once([XI[0]], [xi_1])
+        halves(ETA[:2], eta_1)
         halves(ITEM_3, item_3)
         halves(ITEM_4, item_4)
         at(REDUCE_3, reduce_3)
-        once([XI[1]] + ETA[1:], [xi_2, eta_2, eta_3])
+        once([XI[1]] + ETA[2:], [xi_2, eta_2, eta_3])
         return carry
 
     lax.fori_loop(0, SLOTS, slot_step, 0)
@@ -650,7 +656,7 @@
             V((32, 256, 256), BF16),
             V((8, 8, 256, 128), BF16),
             V((2, 4, 4, 64, 512), BF16),
-            V((2, 256, 512), BF16),
+            V((512, 1024), BF16),
             V((2, 4, 4, 64, 512), F32),
             V((8, 8, 256, 128), F32),
             V((8, 4, 2, 256, 128), BF16),

time: 70.3 us -> 67.1 us (0.954)
  Pallas kernels: 68.8 us -> 65.6 us
    pallas_call x1, Pallas kernels: 66.7 us -> 63.5 us  [on_device(): pl.pallas_call(kernel, out_shape=(V((8, 256, 128), F32), V((64, 1024), F3...]
where the time goes in v3:
time: 67.1 us; the launch traced here: 67 us
  Pallas kernels  65.6 us (98%)
  between operations  1.32 us (2%)
    pallas_call x1, Pallas kernels, on_device(): pl.pallas_call(kernel, out_shape=(V((8, 256, 128), F32), V((64, 1024), F3...  63.5 us
    pallas_call x1, Pallas kernels, on_device(): pl.pallas_call(write_out, out_shape=(out((8, 256, 128), F32), out((8, 256...  2.11 us

profile of v3, /device:TPU:0, one launch (start us, length us, event | category | flops | bytes accessed | tf_op | source)
XLA Modules:
  0.0 67.0 jit_solution(18270656933793375557)
XLA Ops:
  1.3 0.0 copy-start
  1.3 0.0 copy-start.1
  1.3 63.5 %update.1 = (f32[8,256,128]{2,1,0:T(8,128)S(1)}, f32[64,1024]{1,0:T(8,128)S(1)}, f32[8,2,128]{2,1,0:T(2,128)S(1)}, f32[2,1,512]{2,1,0:T(1,128)S(1)}, f32[2,8,128]{2,1,0:T(8,128)S(1)}) custom-call(s32[32]{0:T(128)} %bitcast.25, s32[1,1]{1,0:T(1,128)S(6)} %copy.15.live_ref, f32[2048,128]{1,0:T(8,128)} %th_s.1, f32[2048,128]{1,0:T(8,128)} %th_r.1, ...), custom_call_target="tpu_custom_call" | custom-call | flops 12999999488 | bytes 10485760 | tf_op jit(solution)/shard_map/update/pallas_call | solution.py:640
  64.8 0.0 copy-done
  64.8 0.0 copy-done.1
  64.8 2.1 %write_out.1 = (f32[8,256,128]{2,1,0:T(8,128)}, f32[8,256,128]{2,1,0:T(8,128)}, f32[8,2,128]{2,1,0:T(2,128)}, f32[64,1024]{1,0:T(8,128)}, f32[64,1024]{1,0:T(8,128)}, /*index=5*/f32[2,1,512]{2,1,0:T(1,128)}) custom-call(f32[8,256,128]{2,1,0:T(8,128)S(1)} %get-tuple-element.17.user_new, f32[64,1024]{1,0:T(8,128)S(1)} %get-tuple-element.18.item_new, ...), custom_call_target="tpu_custom_call" | custom-call | tf_op jit(solution)/shard_map/write_out/pallas_call | solution.py:712
Async XLA Ops:
  1.3 63.5 %copy-start = (f32[2048]{0:T(1024)S(1)}, f32[2048]{0:T(1024)}, u32[]{:S(2)}) copy-start(f32[2048]{0:T(1024)} %param.11) | copy-start | bytes 24580
  1.3 63.5 %copy-start.1 = (f32[1024]{0:T(1024)S(1)}, f32[1024]{0:T(1024)}, u32[]{:S(2)}) copy-start(f32[1024]{0:T(1024)} %param.14) | copy-start | bytes 12292

commit v4 on v3

--- a/solution.py
+++ b/solution.py
@@ -20,22 +20,22 @@
 BF16 = jnp.bfloat16
 MESH = pl.DeviceIdType.MESH
 OWN = [0, 1, 2, 4, 5, 6, 7, 9]
-FORWARD_1 = [4, 5, 6, 7, 9, 11, 12, 14]
-FORWARD_2 = [7, 9, 11, 12, 14, 15, 16, 17]
-TILES = [13, 14, 15, 16]
-FIRST_HALF = [17, 19]
-SECOND_HALF = [21, 22, 23, 24]
+FORWARD_1 = [4, 5, 6, 7, 9, 11, 13, 14]
+FORWARD_2 = [7, 9, 12, 13, 14, 15, 16, 17]
+TILES = [15, 16]
+FIRST_HALF = [12, 17, 19]
+SECOND_HALF = [13, 14, 21, 22, 23, 24]
 REDUCE_1 = [15, 16, 17, 19, 24, 25, 26, 27]
 REDUCE_2 = [17, 19, 21, 22, 27, 28, 29, 30]
 REDUCE_3 = [21, 23, 25, 26, 31, 32, 33, 34]
 BETA_2 = [4, 5]
 BETA_3 = [8, 10]
-BETA_4 = [13, 13]
+BETA_4 = [12, 13]
 ITEM_1 = [19, 24]
-ITEM_2 = [24, 28]
-ITEM_3 = [30, 32]
+ITEM_2 = [24, 27]
+ITEM_3 = [29, 31]
 ITEM_4 = [33, 35]
-ETA = [26, 29, 31, 34]
+ETA = [26, 28, 31, 34]
 XI = [25, 32]
 TOTAL_BETA = [6, 8, 12]
 TOTAL_THETA = [10, 14, 16, 19]
@@ -327,7 +327,8 @@
         XIP[u] = jnp.concatenate(rows, axis=0)
         sib(u).start()
 
-    def tiles(u):
+    def tiles(n):
+        u = n + 2
         gathered(u)
         t_blocks = factors(u, 1)
         t_all = jnp.concatenate(t_blocks, axis=1)
@@ -337,7 +338,7 @@
         item_terms(1, t_blocks, (0, 1))
 
     def tiles_first(n):
-        u, w = 4 + 2 * n, 2
+        u, w = 2 * n + 2 * (n >= 1).astype(jnp.int32), 2
         for i in range(w):
             gathered(u + i)
         t_blocks = factors(u, w)
@@ -350,7 +351,7 @@
         item_terms(w, t_blocks, (0,))
 
     def tiles_second(n):
-        u = 4 + n
+        u = n + 2 * (n >= 2).astype(jnp.int32)
         t_blocks = factors(u, 1)
         ratios(u, 1, 1, jnp.concatenate(t_blocks, axis=1))
 

time: 67.1 us -> 65.6 us (0.978)
  Pallas kernels: 65.6 us -> 64.1 us
    pallas_call x1, Pallas kernels: 63.5 us -> 62 us  [on_device(): pl.pallas_call(kernel, out_shape=(V((8, 256, 128), F32), V((64, 1024), F3...]
where the time goes in v4:
time: 65.6 us; the launch traced here: 65.5 us
  Pallas kernels  64.1 us (98%)
  between operations  1.32 us (2%)
    pallas_call x1, Pallas kernels, on_device(): pl.pallas_call(kernel, out_shape=(V((8, 256, 128), F32), V((64, 1024), F3...  62 us
    pallas_call x1, Pallas kernels, on_device(): pl.pallas_call(write_out, out_shape=(out((8, 256, 128), F32), out((8, 256...  2.11 us

profile of v4, /device:TPU:0, one launch (start us, length us, event | category | flops | bytes accessed | tf_op | source)
XLA Modules:
  0.0 65.5 jit_solution(1097745420636703260)
XLA Ops:
  1.3 0.0 copy-start
  1.3 0.0 copy-start.1
  1.3 62.0 %update.1 = (f32[8,256,128]{2,1,0:T(8,128)S(1)}, f32[64,1024]{1,0:T(8,128)S(1)}, f32[8,2,128]{2,1,0:T(2,128)S(1)}, f32[2,1,512]{2,1,0:T(1,128)S(1)}, f32[2,8,128]{2,1,0:T(8,128)S(1)}) custom-call(s32[32]{0:T(128)} %bitcast.25, s32[1,1]{1,0:T(1,128)S(6)} %copy.15.live_ref, f32[2048,128]{1,0:T(8,128)} %th_s.1, f32[2048,128]{1,0:T(8,128)} %th_r.1, ...), custom_call_target="tpu_custom_call" | custom-call | flops 12999999488 | bytes 10485760 | tf_op jit(solution)/shard_map/update/pallas_call | solution.py:641
  63.3 0.0 copy-done
  63.3 0.0 copy-done.1
  63.3 2.1 %write_out.1 = (f32[8,256,128]{2,1,0:T(8,128)}, f32[8,256,128]{2,1,0:T(8,128)}, f32[8,2,128]{2,1,0:T(2,128)}, f32[64,1024]{1,0:T(8,128)}, f32[64,1024]{1,0:T(8,128)}, /*index=5*/f32[2,1,512]{2,1,0:T(1,128)}) custom-call(f32[8,256,128]{2,1,0:T(8,128)S(1)} %get-tuple-element.17.user_new, f32[64,1024]{1,0:T(8,128)S(1)} %get-tuple-element.18.item_new, ...), custom_call_target="tpu_custom_call" | custom-call | tf_op jit(solution)/shard_map/write_out/pallas_call | solution.py:713
Async XLA Ops:
  1.3 62.0 %copy-start = (f32[2048]{0:T(1024)S(1)}, f32[2048]{0:T(1024)}, u32[]{:S(2)}) copy-start(f32[2048]{0:T(1024)} %param.11) | copy-start | bytes 24580
  1.3 62.0 %copy-start.1 = (f32[1024]{0:T(1024)S(1)}, f32[1024]{0:T(1024)}, u32[]{:S(2)}) copy-start(f32[1024]{0:T(1024)} %param.14) | copy-start | bytes 12292
